TPU v7x, 256 devices: a whole 4x4x8 slice. The times are simulated.
256 devices in a mesh: lend: 32 (over z, x), tp: 8 (over y, core).
Axes of the slice: x: 4, y: 4, z: 8, core: 2. Of those that a mesh axis runs over, the one named last changes fastest.
Arguments:
- queries: bfloat16 [512, 8, 64, 128], P(('lend', 'tp')), may hold values from -8 to 8
- new_keys: bfloat16 [512, 8, 4, 128], P(('lend', 'tp')), may hold values from -12 to 12
- new_values: bfloat16 [512, 8, 4, 128], P(('lend', 'tp')), may hold values from -6 to 6
- home_keys: bfloat16 [512, 512, 8, 128], P('lend', None, 'tp'), may hold values from -8 to 8
- home_values: bfloat16 [512, 512, 8, 128], P('lend', None, 'tp'), may hold values from -6 to 6
- lent_keys: bfloat16 [1024, 512, 8, 128], P('lend', None, 'tp'), may hold values from -8 to 8
- lent_values: bfloat16 [1024, 512, 8, 128], P('lend', None, 'tp'), may hold values from -6 to 6
- lengths: int32 [512], replicated, may hold values from 1 to 32256, as said below
- slot_owner: int32 [1024], replicated, may hold values from -1 to 511, as said below
Outputs:
- attended: bfloat16 [512, 8, 64, 128], P(('lend', 'tp'))
Inputs may be any that keep to these rules, and one draw needn't show every extreme that they name: `lengths`: request r belongs to home group r // 16. Of its L cached tokens it holds the first min(L, 512) at home; when L > 512 it has exactly ceil((L - 512) / 512) lent blocks in slot_owner, else none. `slot_owner`: slot s lies on lender s // 32. A request's blocks are numbered from 0 in slot order. No block lies on the lender of its request's own home group. On one lender at most 2 slots hold blocks of one home group's requests, and in every draw some lenders hold exactly 2 for some home group.
All inputs are finite; a program needn't handle non-finite values.
Results may differ from a plain program's by a relative error of at most 0.0031.
Values may be sent and summed in bfloat16 or wider, within the bound.
No kernel may reach another device: no remote copies, remote signals or barrier semaphores. Data moves between devices by JAX's collectives and lax.ppermute only.
A program may use at most 64 MiB of HBM per device.

v0:
```python
import math

import jax
import jax.numpy as jnp
from jax import lax
from jax.sharding import PartitionSpec as P

STEPS = 4
CAP = 2
HOME_CAP = 512
BLOCK = 512


NEG_BIG = -1e30


def home_part(queries, new_keys, new_values, home_keys, home_values, home_lengths):
    factor = 1.0 / math.sqrt(queries.shape[-1])
    row_count = queries.shape[2]
    group_size = row_count // STEPS
    home_scores = (
        jnp.einsum("ikqd,ijkd->ikqj", queries, home_keys, preferred_element_type=jnp.float32)
        * factor
    )
    new_scores = (
        jnp.einsum("ikqd,iktd->ikqt", queries, new_keys, preferred_element_type=jnp.float32)
        * factor
    )
    home_visible = (
        jnp.arange(home_keys.shape[1])[None, :] < jnp.minimum(home_lengths, HOME_CAP)[:, None]
    )[:, None, None, :]
    new_visible = (jnp.arange(STEPS)[None, :] <= (jnp.arange(row_count) // group_size)[:, None])[
        None, None
    ]
    home_masked = jnp.where(home_visible, home_scores, NEG_BIG)
    new_masked = jnp.where(new_visible, new_scores, NEG_BIG)
    top_score = jnp.maximum(jnp.max(home_masked, axis=-1), jnp.max(new_masked, axis=-1))
    home_terms = jnp.where(home_visible, jnp.exp(home_masked - top_score[..., None]), 0.0)
    new_terms = jnp.where(new_visible, jnp.exp(new_masked - top_score[..., None]), 0.0)
    row_total = jnp.sum(home_terms, axis=-1) + jnp.sum(new_terms, axis=-1)
    mixture = jnp.einsum(
        "ikqj,ijkd->ikqd",
        home_terms.astype(jnp.bfloat16),
        home_values,
        preferred_element_type=jnp.float32,
    )
    mixture = mixture + jnp.einsum(
        "ikqt,iktd->ikqd",
        new_terms.astype(jnp.bfloat16),
        new_values,
        preferred_element_type=jnp.float32,
    )
    return (mixture / row_total[..., None], top_score + jnp.log(row_total))


def lent_part(slot_queries, lent_keys, lent_values, visible):
    factor = 1.0 / math.sqrt(slot_queries.shape[-1])
    scores = (
        jnp.einsum("skqd,sjkd->skqj", slot_queries, lent_keys, preferred_element_type=jnp.float32)
        * factor
    )
    spread = visible[:, None, None, :]
    masked = jnp.where(spread, scores, NEG_BIG)
    top_score = jnp.max(masked, axis=-1)
    exp_terms = jnp.where(spread, jnp.exp(masked - top_score[..., None]), 0.0)
    filled = jnp.any(visible, axis=1)[:, None, None]
    divisor = jnp.where(filled, jnp.sum(exp_terms, axis=-1), 1.0)
    lent_out = jnp.einsum(
        "skqj,sjkd->skqd",
        exp_terms.astype(jnp.bfloat16),
        lent_values,
        preferred_element_type=jnp.float32,
    )
    return (lent_out / divisor[..., None], top_score + jnp.log(divisor))


def shards(
    queries,
    new_keys,
    new_values,
    home_keys,
    home_values,
    lent_keys,
    lent_values,
    lengths,
    slot_owner,
):
    queries_home, keys_new, values_new = (
        lax.all_to_all(queries, "tp", split_axis=1, concat_axis=0, tiled=True),
        lax.all_to_all(new_keys, "tp", split_axis=1, concat_axis=0, tiled=True),
        lax.all_to_all(new_values, "tp", split_axis=1, concat_axis=0, tiled=True),
    )
    lend_count = lax.axis_size("lend")
    lend_index = lax.axis_index("lend")
    req_count = queries_home.shape[0]
    slot_count = lent_keys.shape[0]
    place_count = lend_count * CAP
    home_lengths = lax.dynamic_slice_in_dim(lengths, lend_index * req_count, req_count)
    home_out, home_lse = home_part(
        queries_home, keys_new, values_new, home_keys, home_values, home_lengths
    )
    owner_table = slot_owner.reshape(lend_count, slot_count)
    home_table = jnp.where(owner_table >= 0, owner_table // req_count, -1)
    position = jnp.arange(slot_count)
    earlier = position[None, :] < position[:, None]
    rank_table = jnp.sum(
        ((home_table[:, :, None] == home_table[:, None, :]) & earlier[None]).astype(jnp.int32),
        axis=2,
    )
    picked = (home_table[:, None, :] == lend_index) & (
        rank_table[:, None, :] == jnp.arange(CAP)[None, :, None]
    )
    present = jnp.any(picked, axis=2).reshape(-1)
    local_owner = jnp.sum(
        jnp.where(picked, owner_table[:, None, :] - lend_index * req_count, 0), axis=2
    ).reshape(-1)
    own_owner = lax.dynamic_slice_in_dim(slot_owner, lend_index * slot_count, slot_count)
    own_filled = own_owner >= 0
    own_home = jnp.where(own_filled, own_owner // req_count, 0)
    own_rank = lax.dynamic_index_in_dim(rank_table, lend_index, 0, keepdims=False)
    flat_place = jnp.clip(own_home * CAP + own_rank, 0, place_count - 1)
    slot_number = lend_index * slot_count + position
    all_positions = jnp.arange(slot_owner.shape[0])
    block_id = jnp.sum(
        (
            (slot_owner[None, :] == own_owner[:, None])
            & (all_positions[None, :] < slot_number[:, None])
        ).astype(jnp.int32),
        axis=1,
    )
    owner_length = jnp.take(lengths, jnp.maximum(own_owner, 0), axis=0)
    visible = own_filled[:, None] & (
        HOME_CAP + block_id[:, None] * BLOCK + jnp.arange(lent_keys.shape[1])[None, :]
        < owner_length[:, None]
    )
    matched = (flat_place[None, :] == jnp.arange(place_count)[:, None]) & own_filled[None, :]
    back_index = jnp.sum(jnp.where(matched, position[None, :], 0), axis=1)
    gathered = lax.all_gather(queries_home, "lend", axis=0, tiled=True)
    slot_queries = jnp.take(gathered, jnp.maximum(own_owner, 0), axis=0)
    lent_out, lent_lse = lent_part(slot_queries, lent_keys, lent_values, visible)
    placed_out = jnp.take(lent_out, back_index, axis=0)
    placed_lse = jnp.take(lent_lse, back_index, axis=0)
    returned_out, returned_lse = lax.all_to_all(
        (
            placed_out.reshape((lend_count, CAP) + placed_out.shape[1:]),
            placed_lse.reshape((lend_count, CAP) + placed_lse.shape[1:]),
        ),
        "lend",
        split_axis=0,
        concat_axis=0,
        tiled=True,
    )
    flat_out = returned_out.reshape((place_count,) + returned_out.shape[2:])
    flat_lse = returned_lse.reshape((place_count,) + returned_lse.shape[2:])
    belongs = present[:, None] & (local_owner[:, None] == jnp.arange(req_count)[None, :])
    member = belongs[:, :, None, None]
    lse_spread = jnp.where(member, flat_lse[:, None], NEG_BIG)
    top_score = jnp.maximum(home_lse, jnp.max(lse_spread, axis=0))
    coefficient = jnp.where(
        member,
        jnp.exp(jnp.where(member, flat_lse[:, None], top_score[None]) - top_score[None]),
        0.0,
    )
    home_coefficient = jnp.exp(home_lse - top_score)
    row_total = home_coefficient + jnp.sum(coefficient, axis=0)
    mixture = home_coefficient[..., None] * home_out + jnp.einsum(
        "pikq,pkqd->ikqd", coefficient, flat_out, precision=lax.Precision.HIGHEST
    )
    attended = (mixture / row_total[..., None]).astype(jnp.bfloat16)
    return lax.all_to_all(attended, "tp", split_axis=0, concat_axis=1, tiled=True)


def solution(mesh):
    return jax.shard_map(
        shards,
        mesh=mesh,
        in_specs=(
            P(("lend", "tp"), None, None, None),
            P(("lend", "tp"), None, None, None),
            P(("lend", "tp"), None, None, None),
            P("lend", None, "tp", None),
            P("lend", None, "tp", None),
            P("lend", None, "tp", None),
            P("lend", None, "tp", None),
            P(),
            P(),
        ),
        out_specs=P(("lend", "tp"), None, None, None),
        check_vma=False,
    )
```

profile of v0, /device:TPU:1, one launch (start us, length us, event | category | flops | bytes accessed | tf_op | source)
XLA Modules:
  0.0 233.8 jit_solution(5230799109210936811)
XLA Ops:
  6.5 0.0 copy-start
  6.5 0.0 all-gather.2.cloned.1.call-start
  6.5 1.1 copy.56
  7.7 12.8 %all_to_all.76 = bf16[2,8,64,128]{3,2,0,1:T(8,128)(2,1)} all-to-all(bf16[2,8,64,128]{3,2,0,1:T(8,128)(2,1)S(1)} %copy.56), channel_id=1, replica_groups=mesh['lend'=32,'tp'=8] {'tp'}, dimensions={1} | all-to-all | bytes 524288 | tf_op jit(solution)/shard_map/all_to_all | solution.py:89
  20.5 0.0 all-gather.2.cloned.1.call-update
  20.5 1.3 copy.57
  21.8 4.3 %all-to-all-start.1 = ((bf16[2,8,4,128]{3,2,0,1:T(4,128)(2,1)}), bf16[2,8,4,128]{3,2,0,1:T(4,128)(2,1)S(1)}, u32[]{:S(2)}, u32[]{:S(2)}) async-start(bf16[2,8,4,128]{3,2,0,1:T(4,128)(2,1)} %copy.57), calls=%async_computation.1 | async-start | bytes 32768 | tf_op jit(solution)/shard_map/all_to_all | solution.py:90
  26.1 0.8 reshape.585
  26.9 0.8 convert_reduce_fusion
  27.7 0.8 fusion.89
  28.5 0.1 select_reduce_fusion.3
  28.6 0.1 reduce_sum.83
  28.7 1.3 copy.63
  30.0 1.4 gather_fusion
  31.4 0.0 copy-done.4
  31.4 0.2 convert_reduce_fusion.1
  31.7 0.2 fusion.99
  31.9 87.4 %all-gather.2.cloned.1.call-done = bf16[512,1,64,128]{3,2,1,0:T(8,128)(2,1)} async-done(((bf16[16,1,64,128]{3,2,1,0:T(8,128)(2,1)}), bf16[512,1,64,128]{3,2,1,0:T(8,128)(2,1)}) %all-gather.2.cloned.1.call-update) | async-done | bytes 8388624 | tf_op jit(solution)/shard_map/all_gather | solution.py:138
  119.3 4.0 %gather_fusion.1 = bf16[32,64,128]{2,1,0:T(8,128)(2,1)S(1)} fusion(bf16[512,64,128]{2,1,0:T(8,128)(2,1)} %bitcast.123, s32[1024]{0:T(1024)S(1)} %pad_clamp_fusion.1), kind=kCustom, calls=%fused_computation.1 | custom fusion | bytes 1048704 | tf_op jit(solution)/shard_map/jit(_take)/gather | solution.py:139
  123.3 3.9 %fusion.4 = (f32[32,64]{1,0:T(8,128)S(1)}, f32[32,64,512]{2,1,0:T(8,128)S(1)}) fusion(pred[32,512]{1,0:T(8,128)(4,1)S(1)} %get-tuple-element.14, bf16[32,512,1,128]{3,1,2,0:T(8,128)(2,1)} %param.14, bf16[32,64,128]{2,1,0:T(8,128)(2,1)S(1)} %gather_fusion.1, pred[32]{0:T(512)(128)(4,1)S(1)} %get-tuple-element.16), kind=kOutput, calls=%fused_computation.10 | convolution fusion | flops 271841280 | bytes 8937504 | tf_op jit(solution)/shard_map/skqd,sjkd->skqj/dot_general | solution.py:59
  127.2 1.7 fusion.6
  128.9 0.1 broadcast_select_fusion.2
  129.0 0.5 copy-done.5
  129.4 1.7 fusion.51
  131.2 0.1 fusion.80
  131.3 0.6 gather_fusion.2
  131.8 0.0 all-to-all-done.1
  131.9 5.4 %all-to-all-start.3 = ((bf16[2,8,4,128]{3,2,0,1:T(4,128)(2,1)}), bf16[2,8,4,128]{3,2,0,1:T(4,128)(2,1)S(1)}, u32[]{:S(2)}, u32[]{:S(2)}) async-start(bf16[2,8,4,128]{3,2,0,1:T(4,128)(2,1)} %copy.63), calls=%async_computation.3 | async-start | bytes 32768 | tf_op jit(solution)/shard_map/all_to_all | solution.py:91
  137.2 0.1 fusion.103
  137.3 0.7 reshape.635
  138.0 2.0 gather_fusion.3
  140.0 1.9 all-to-all-done.3
  141.9 5.4 %all-to-all-start.2 = ((f32[32,1,128]{2,1,0:T(1,128)}), f32[32,1,128]{2,1,0:T(1,128)S(1)}, u32[]{:S(2)}, u32[]{:S(2)}) async-start(f32[32,1,128]{2,1,0:T(1,128)} %reshape.635), calls=%async_computation.2 | async-start | bytes 32768 | tf_op jit(solution)/shard_map/all_to_all | solution.py:143
  147.3 3.2 %broadcast_select_fusion = f32[32,2,1,64,128]{4,3,1,2,0:T(8,128)} fusion(f32[32,2,1,64,128]{4,3,1,2,0:T(8,128)} %bitcast.112, pred[32,2]{1,0:T(8,128)(4,1)S(1)} %compare_and_fusion), kind=kLoop, calls=%fused_computation.37 | loop fusion | flops 524288 | bytes 4194368 | tf_op jit(solution)/shard_map/jit(_take)/select_n | solution.py:141
  150.4 5.3 %all-to-all-done.2 = f32[32,1,128]{2,1,0:T(1,128)S(1)} async-done(((f32[32,1,128]{2,1,0:T(1,128)}), f32[32,1,128]{2,1,0:T(1,128)S(1)}, u32[]{:S(2)}, u32[]{:S(2)}) %all-to-all-start.2) | async-done | bytes 16416 | tf_op jit(solution)/shard_map/all_to_all | solution.py:143
  155.7 4.9 %all-to-all-start.4 = ((f32[32,2,1,64,128]{4,3,1,2,0:T(8,128)}), f32[32,2,1,64,128]{4,3,1,2,0:T(8,128)}, u32[]{:S(2)}, u32[]{:S(2)}) async-start(f32[32,2,1,64,128]{4,3,1,2,0:T(8,128)} %broadcast_select_fusion), calls=%async_computation.4 | async-start | bytes 4194304 | tf_op jit(solution)/shard_map/all_to_all | solution.py:143
  160.6 0.1 select_reduce_fusion.2
  160.8 0.1 copy.59
  160.9 0.1 eq.90
  161.0 0.1 fusion.71
  161.1 0.1 copy.58
  161.2 0.1 and.122
  161.3 0.1 copy.60
  161.4 0.8 dynamic-slice_minimum_fusion
  162.2 0.1 iota_compare_fusion.2
  162.3 0.0 copy-done.3
  162.3 0.3 fusion.102
  162.6 0.9 fusion.17
  163.6 0.3 fusion.74
  163.8 1.0 copy-done.1
  164.8 0.8 fusion.19
  165.6 0.5 broadcast.485
  166.1 0.7 reduce.14
  166.8 0.1 reshape.636
  166.9 0.1 copy.66
  167.0 0.2 select_reduce_fusion.1
  167.2 0.1 copy.67
  167.3 0.2 select_reduce_fusion
  167.5 38.5 %all-to-all-done.4 = f32[32,2,1,64,128]{4,3,1,2,0:T(8,128)} async-done(((f32[32,2,1,64,128]{4,3,1,2,0:T(8,128)}), f32[32,2,1,64,128]{4,3,1,2,0:T(8,128)}, u32[]{:S(2)}, u32[]{:S(2)}) %all-to-all-start.4) | async-done | bytes 2097184 | tf_op jit(solution)/shard_map/all_to_all | solution.py:143
  206.0 3.4 %copy.65 = f32[32,2,1,64,128]{4,1,0,3,2:T(2,128)S(1)} copy(f32[32,2,1,64,128]{4,3,1,2,0:T(8,128)} %all-to-all-done.4) | data formatting | bytes 4194304 | tf_op jit(solution)/shard_map/all_to_all | solution.py:143
  209.4 2.0 fusion.56
  211.4 1.2 fusion.41
  212.7 13.6 %all_to_all.77 = bf16[16,1,64,128]{3,2,1,0:T(8,128)(2,1)S(1)} all-to-all(bf16[16,1,64,128]{3,2,1,0:T(8,128)(2,1)S(1)} %fusion.41), channel_id=1, replica_groups=mesh['lend'=32,'tp'=8] {'tp'}, dimensions={0} | all-to-all | bytes 524288 | tf_op jit(solution)/shard_map/all_to_all | solution.py:170
  226.3 0.7 copy.73
  (27 shorter events, 0.2 us)
Async XLA Ops:
  6.5 156.0 %copy-start = (bf16[16,512,1,128]{3,1,2,0:T(8,128)(2,1)S(1)}, bf16[16,512,1,128]{3,1,2,0:T(8,128)(2,1)}, u32[]{:S(2)}) copy-start(bf16[16,512,1,128]{3,1,2,0:T(8,128)(2,1)} %param.12) | copy-start | bytes 6291460
  6.5 24.9 %copy-start.4 = (s32[1024]{0:T(1024)S(1)}, s32[1024]{0:T(1024)}, u32[]{:S(2)}) copy-start(s32[1024]{0:T(1024)} %param.17) | copy-start | bytes 12292
  6.5 112.7 %all-gather.2.cloned.1.call-start = ((), (), s32[]{:S(2)}) async-start(), calls=%async_computation.6 | async-start | bytes 8650752 | tf_op jit(solution)/shard_map/all_gather | solution.py:138
  21.8 110.0 %all-to-all-start.1 = ((bf16[2,8,4,128]{3,2,0,1:T(4,128)(2,1)}), bf16[2,8,4,128]{3,2,0,1:T(4,128)(2,1)S(1)}, u32[]{:S(2)}, u32[]{:S(2)}) async-start(bf16[2,8,4,128]{3,2,0,1:T(4,128)(2,1)} %copy.57), calls=%async_computation.1 | async-start | bytes 32768 | tf_op jit(solution)/shard_map/all_to_all | solution.py:90
  127.2 2.2 copy-start.5
  131.9 10.0 %all-to-all-start.3 = ((bf16[2,8,4,128]{3,2,0,1:T(4,128)(2,1)}), bf16[2,8,4,128]{3,2,0,1:T(4,128)(2,1)S(1)}, u32[]{:S(2)}, u32[]{:S(2)}) async-start(bf16[2,8,4,128]{3,2,0,1:T(4,128)(2,1)} %copy.63), calls=%async_computation.3 | async-start | bytes 32768 | tf_op jit(solution)/shard_map/all_to_all | solution.py:91
  141.9 13.8 %all-to-all-start.2 = ((f32[32,1,128]{2,1,0:T(1,128)}), f32[32,1,128]{2,1,0:T(1,128)S(1)}, u32[]{:S(2)}, u32[]{:S(2)}) async-start(f32[32,1,128]{2,1,0:T(1,128)} %reshape.635), calls=%async_computation.2 | async-start | bytes 32768 | tf_op jit(solution)/shard_map/all_to_all | solution.py:143
  150.4 11.9 %copy-start.3 = (bf16[2,8,64,128]{3,2,0,1:T(8,128)(2,1)S(1)}, bf16[2,8,64,128]{3,2,0,1:T(8,128)(2,1)}, u32[]{:S(2)}) copy-start(bf16[2,8,64,128]{3,2,0,1:T(8,128)(2,1)} %all_to_all.76) | copy-start | bytes 786436
  155.7 50.4 %all-to-all-start.4 = ((f32[32,2,1,64,128]{4,3,1,2,0:T(8,128)}), f32[32,2,1,64,128]{4,3,1,2,0:T(8,128)}, u32[]{:S(2)}, u32[]{:S(2)}) async-start(f32[32,2,1,64,128]{4,3,1,2,0:T(8,128)} %broadcast_select_fusion), calls=%async_computation.4 | async-start | bytes 4194304 | tf_op jit(solution)/shard_map/all_to_all | solution.py:143
  163.5 1.3 copy-start.1
  206.0 5.4 %copy-start.6 = (bf16[16,512,1,128]{3,1,2,0:T(8,128)(2,1)S(1)}, bf16[16,512,1,128]{3,1,2,0:T(8,128)(2,1)}, u32[]{:S(2)}) copy-start(bf16[16,512,1,128]{3,1,2,0:T(8,128)(2,1)} %param.13) | copy-start | bytes 6291460
  209.4 2.0 copy-start.2
Sparse Core Ops, SparseCore 0:
  20.6 98.6 all-gather.1
where the time goes:
time: 236 us; the launch traced here: 234 us
  waiting for transfers between devices  133 us (56%)
  blocking collectives  26.4 us (11%)
  local copies, waits for them, and re-layouts  20.2 us (9%)
  starting transfers between devices  20 us (8%)
  between operations  13.7 us (6%)
  matrix products  10.3 us (4%)
  other arithmetic  10.2 us (4%)
    all_gather x1, waiting for transfers between devices, shards(): gathered = lax.all_gather(queries_home, 'lend', axis=0, tiled=True)  87.4 us
    all_to_all x2, waiting for transfers between devices, shards(): lax.all_to_all((placed_out.reshape((lend_count, CAP) + placed_out.shape[1...  43.8 us
    all_to_all x1, blocking collectives, shards(): lax.all_to_all(attended, 'tp', split_axis=0, concat_axis=1, tiled=True)  13.6 us
    all_to_all x1, blocking collectives, shards(): lax.all_to_all(queries, 'tp', split_axis=1, concat_axis=0, tiled=True)  12.8 us
    all_to_all x2, starting transfers between devices, shards(): lax.all_to_all((placed_out.reshape((lend_count, CAP) + placed_out.shape[1...  10.3 us
    unnamed x19, local copies, waits for them, and re-layouts  6.03 us
    all_to_all x1, starting transfers between devices, shards(): lax.all_to_all(new_values, 'tp', split_axis=1, concat_axis=0, tiled=True)  5.38 us
  transfers between devices with their start and end apart: 5, of which 4 were waited for; matrix products, arithmetic and copies ran while one was open for 13% of the time, Pallas kernels for 0%

commit v1 on v0

v1 whole, which is shorter than its diff:
```python
import math

import jax
import jax.numpy as jnp
from jax import lax
from jax.experimental import pallas as pl
from jax.experimental.pallas import tpu as pltpu
from jax.sharding import PartitionSpec as P

STEPS = 4
CAP = 2
HOME_CAP = 512
BLOCK = 512
STAT_ROWS = 8
LANES = 128
LENT_GROUP = 8
HOME_GROUP = 2
MERGE_GROUP = 4
LENT_MIB = 58

NEG_BIG = -1e30
FAR = 1 << 30
LOG2E = math.log2(math.e)

VMEM = pltpu.VMEM
SMEM = pltpu.SMEM
HBM = pltpu.HBM


def spec(space):
    return pl.BlockSpec(memory_space=space)


def nt_dot(left, right):
    return lax.dot_general(
        left, right, (((1,), (1,)), ((), ())), preferred_element_type=jnp.float32
    )


def nn_dot(left, right):
    return lax.dot_general(
        left, right, (((1,), (0,)), ((), ())), preferred_element_type=jnp.float32
    )


def pack_kernel(queries, new_keys, new_values, out, news, sems):
    per_source, heads, rows, _ = queries.shape
    fresh = [
        pltpu.make_async_copy(new_keys, news.at[0], sems.at[0]),
        pltpu.make_async_copy(new_values, news.at[1], sems.at[1]),
    ]
    copies = [
        pltpu.make_async_copy(
            queries.at[part], out.at[:, part * rows : (part + 1) * rows], sems.at[2 + part]
        )
        for part in range(per_source)
    ]
    for copy in fresh + copies:
        copy.start()
    for copy in fresh:
        copy.wait()
    for head in range(heads):
        block = [news[kind, part, head] for kind in range(2) for part in range(per_source)]
        block = jnp.concatenate([array.astype(jnp.float32) for array in block], axis=0)
        out[head, per_source * rows :, :] = block.astype(jnp.bfloat16)
    for copy in copies:
        copy.wait()


def pick_kernel(starts, packed_ref, out_ref, *, rows):
    for place in range(out_ref.shape[0] * CAP):
        lender, rank = divmod(place, CAP)
        start = pl.multiple_of(starts[place], 16)
        out_ref[lender, rank * rows : (rank + 1) * rows, :] = packed_ref[pl.ds(start, rows), :]


def home_kernel(
    info, packed_ref, keys, values, tables, asked, out_ref, lse_ref, stats, *, rows, per_source
):
    sources = packed_ref.shape[0]
    requests = sources * per_source
    new_start = rows * per_source
    new_half = STEPS * per_source
    factor = 1.0 / math.sqrt(packed_ref.shape[-1])

    stats[...] = jnp.zeros_like(stats)
    token = lax.broadcasted_iota(jnp.int32, (rows, new_half), 1)
    step = lax.broadcasted_iota(jnp.int32, (rows, new_half), 0) // (rows // STEPS)
    lane = lax.broadcasted_iota(jnp.int32, stats.shape, 1)

    def some(group, carry):
        chosen = [
            (group * HOME_GROUP + near, part)
            for near in range(HOME_GROUP)
            for part in range(per_source)
        ]
        scores, new_scores, mixed, total = [], [], [], []
        news = []
        for source, part in chosen:
            request = source * per_source + part
            query = packed_ref[source, part * rows : (part + 1) * rows, :]
            block = packed_ref[source, new_start : new_start + 2 * new_half, :].astype(jnp.float32)
            new_keys = block[:new_half].astype(jnp.bfloat16)
            news.append(block[new_half:].astype(jnp.bfloat16))
            length = jnp.minimum(info[request], HOME_CAP)
            raw = nt_dot(query, keys[request])
            position = lax.broadcasted_iota(jnp.int32, raw.shape, 1)
            scores.append(jnp.where(position < length, raw, NEG_BIG))
            seen = (token >= part * STEPS) & (token - part * STEPS <= step)
            seen = seen & (token < (part + 1) * STEPS)
            new_scores.append(jnp.where(seen, nt_dot(query, new_keys), NEG_BIG))
        tops = [
            jnp.maximum(jnp.max(old, axis=1, keepdims=True), jnp.max(new, axis=1, keepdims=True))
            for old, new in zip(scores, new_scores)
        ]
        for near, (source, part) in enumerate(chosen):
            terms = jnp.exp2((scores[near] - tops[near]) * (factor * LOG2E))
            new_terms = jnp.exp2((new_scores[near] - tops[near]) * (factor * LOG2E))
            total.append(
                jnp.sum(terms, axis=1, keepdims=True) + jnp.sum(new_terms, axis=1, keepdims=True)
            )
            mixed.append(
                nn_dot(terms.astype(jnp.bfloat16), values[source * per_source + part])
                + nn_dot(new_terms.astype(jnp.bfloat16), news[near])
            )
        collected = stats[...]
        for near, (source, part) in enumerate(chosen):
            request = source * per_source + part
            out_ref[request] = mixed[near] * (1.0 / total[near])
            collected = jnp.where(
                lane == request, tops[near] * factor + jnp.log(total[near]), collected
            )
        stats[...] = collected
        return carry

    lax.fori_loop(0, sources // HOME_GROUP, some, 0)
    turned = stats[...].T[:requests]
    lse_ref[...] = jnp.concatenate([turned] * CAP, axis=1)


def lent_kernel(
    info,
    query_hbm,
    keys_hbm,
    values_hbm,
    home_lse,
    out_ref,
    queries,
    keys,
    values,
    stats,
    sems,
    *,
    rows,
):
    slots = keys_hbm.shape[0]
    homes = query_hbm.shape[0]
    group = min(LENT_GROUP, slots)
    chunks = slots // group
    factor = 1.0 / math.sqrt(query_hbm.shape[-1])

    def copy(kind, chunk):
        source, target = ((keys_hbm, keys), (values_hbm, values))[kind]
        part = pl.ds(chunk * group, group)
        return pltpu.make_async_copy(source.at[part], target.at[part], sems.at[chunk, kind])

    arrival = pltpu.make_async_copy(query_hbm, queries, sems.at[chunks, 0])
    arrival.start()
    for chunk in range(chunks):
        for kind in range(2):
            copy(kind, chunk).start()
    stats[...] = jnp.zeros_like(stats)
    lane = lax.broadcasted_iota(jnp.int32, (rows, stats.shape[1]), 1)
    arrival.wait()

    def some(chunk, carry):
        for kind in range(2):
            copy(kind, chunk).wait()
        scores, placed, mixed, total = [], [], [], []
        for near in range(group):
            slot = chunk * group + near
            place = info[slot]
            length = info[slots + slot]
            home = lax.div(place, CAP)
            start = pl.multiple_of(lax.rem(place, CAP) * rows, rows)
            raw = nt_dot(queries[home, pl.ds(start, rows), :], keys[slot])
            position = lax.broadcasted_iota(jnp.int32, raw.shape, 1)
            scores.append(jnp.where(position < length, raw, NEG_BIG))
            placed.append((home, start))
        tops = [jnp.max(old, axis=1, keepdims=True) for old in scores]
        for near in range(group):
            terms = jnp.exp2((scores[near] - tops[near]) * (factor * LOG2E))
            total.append(jnp.sum(terms, axis=1, keepdims=True))
            mixed.append(nn_dot(terms.astype(jnp.bfloat16), values[chunk * group + near]))
        for near, (home, start) in enumerate(placed):
            out_ref[home, pl.ds(start, rows), :] = (mixed[near] * (1.0 / total[near])).astype(
                jnp.bfloat16
            )
            stats[pl.ds(start, rows), :] = jnp.where(
                lane == home,
                tops[near] * factor + jnp.log(total[near]),
                stats[pl.ds(start, rows), :],
            )
        return carry

    lax.fori_loop(0, chunks, some, 0)
    turned = stats[...].T[:homes]
    high = turned.astype(jnp.bfloat16).astype(jnp.float32)
    middle = (turned - high).astype(jnp.bfloat16).astype(jnp.float32)
    low = turned - high - middle
    shape = (homes, STAT_ROWS, CAP * rows)
    row = lax.broadcasted_iota(jnp.int32, shape, 1)
    packed = jnp.where(
        row == 0,
        high[:, None, :],
        jnp.where(row == 1, middle[:, None, :], jnp.where(row == 2, low[:, None, :], 0.0)),
    )
    out_ref[:, CAP * rows :, :] = packed.astype(jnp.bfloat16)


def combine_kernel(
    info, picks_wide, back_ref, home_out, home_lse, out_ref, mixed, wide, *, rows
):
    lenders = back_ref.shape[0]
    requests = home_out.shape[0]
    count = out_ref.shape[0]
    per_target = requests // count

    lse = jnp.sum(back_ref[:, CAP * rows :, :].astype(jnp.float32), axis=1)
    owner = picks_wide[...]
    belongs = [owner == request for request in range(requests)]

    def per_request(values, reduce, other):
        parts = [
            reduce(jnp.where(mask, values, other), axis=0, keepdims=True) for mask in belongs
        ]
        return jnp.concatenate(parts, axis=0)

    def per_place(values, other):
        result = jnp.full(owner.shape, other, jnp.float32)
        for request, mask in enumerate(belongs):
            result = jnp.where(mask, values[request : request + 1], result)
        return result

    local = home_lse[...]
    tops = per_request(lse, jnp.max, NEG_BIG)
    tops = jnp.maximum(jnp.maximum(tops, pltpu.roll(tops, rows, 1)), local)
    weights = jnp.where(owner >= 0, jnp.exp(lse - per_place(tops, 0.0)), 0.0)
    sums = per_request(weights, jnp.sum, 0.0)
    home_weights = jnp.exp(local - tops)
    inverse = 1.0 / (home_weights + sums + pltpu.roll(sums, rows, 1))
    weights = weights * per_place(inverse, 1.0)
    home_weights = home_weights * inverse
    turned = weights.T
    for lender in range(lenders):
        wide[lender] = jnp.broadcast_to(turned[:, lender : lender + 1], wide.shape[1:])
    home_turned = home_weights.T

    for request in range(requests):
        mixed[request] = home_out[request] * home_turned[:rows, request : request + 1]
    filled = info[0]
    places = lenders * CAP

    def some(step, carry):
        terms = []
        for near in range(MERGE_GROUP):
            entry = step * MERGE_GROUP + near
            index = jnp.minimum(entry, filled - 1)
            place = info[1 + index]
            lender = lax.div(place, CAP)
            part = pl.ds(pl.multiple_of(lax.rem(place, CAP) * rows, rows), rows)
            term = wide[lender, part, :] * back_ref[lender, part, :].astype(jnp.float32)
            terms.append((info[1 + places + index], jnp.where(entry < filled, term, 0.0)))
        for request, term in terms:
            mixed[request] = mixed[request] + term
        return carry

    lax.fori_loop(0, lax.div(filled + MERGE_GROUP - 1, MERGE_GROUP), some, 0)
    for target in range(count):
        for part in range(per_target):
            out_ref[target, part * rows : (part + 1) * rows, :] = mixed[
                target * per_target + part
            ].astype(jnp.bfloat16)


def listed(present, columns):
    count = present.shape[0]
    index = jnp.arange(count, dtype=jnp.int32)
    before = index[None, :] < index[:, None]
    position = jnp.sum(present[None, :] & before, axis=1, dtype=jnp.int32)
    chosen = present[None, :] & (position[None, :] == index[:, None])
    parts = [jnp.sum(present, dtype=jnp.int32).reshape(1)]
    parts += [jnp.sum(jnp.where(chosen, column[None, :], 0), axis=1) for column in columns]
    return jnp.concatenate(parts)


def shards(
    queries,
    new_keys,
    new_values,
    home_keys,
    home_values,
    lent_keys,
    lent_values,
    lengths,
    slot_owner,
):
    tp_count = lax.axis_size("tp")
    lend_count = lax.axis_size("lend")
    me = lax.axis_index("lend").astype(jnp.int32)
    per_source, heads, rows, dim = queries.shape
    requests = per_source * tp_count
    slots = lent_keys.shape[0]
    packed_rows = per_source * (rows + 2 * STEPS)

    def params(mib):
        return pltpu.CompilerParams(vmem_limit_bytes=mib << 20)

    packed = pl.pallas_call(
        pack_kernel,
        out_shape=jax.ShapeDtypeStruct((heads, packed_rows, dim), jnp.bfloat16),
        in_specs=[spec(HBM)] * 3,
        out_specs=spec(VMEM),
        scratch_shapes=[
            pltpu.VMEM((2,) + new_keys.shape, jnp.bfloat16),
            pltpu.SemaphoreType.DMA((2 + per_source,)),
        ],
        compiler_params=params(60),
        name="pack",
    )(queries, new_keys, new_values)
    packed = lax.all_to_all(packed, "tp", split_axis=0, concat_axis=0, tiled=True)

    table = slot_owner.reshape(lend_count, slots)
    local = table - me * requests
    code = jnp.where(
        (local >= 0) & (local < requests),
        jnp.arange(slots, dtype=jnp.int32)[None, :] * requests + local,
        FAR,
    )
    first = jnp.min(code, axis=1)
    second = jnp.min(jnp.where(code > first[:, None], code, FAR), axis=1)
    codes = jnp.stack([first, second], axis=1)
    picks_pair = jnp.where(codes < FAR, codes % requests, -1)
    picks = picks_pair.reshape(-1)
    picks_wide = jnp.repeat(picks_pair, rows, axis=1)

    own = lax.dynamic_slice_in_dim(slot_owner, me * slots, slots)
    slot = jnp.arange(slots, dtype=jnp.int32)
    everywhere = jnp.arange(slot_owner.shape[0], dtype=jnp.int32)
    same = slot_owner[None, :] == own[:, None]
    earlier = everywhere[None, :] < (me * slots + slot)[:, None]
    numbers = jnp.sum(same & earlier, axis=1, dtype=jnp.int32)
    request = jnp.arange(lengths.shape[0], dtype=jnp.int32)
    owner_length = jnp.sum(
        jnp.where(request[None, :] == own[:, None], lengths[None, :], 0), axis=1
    )
    length = owner_length - HOME_CAP - numbers * BLOCK
    home = jnp.where(own >= 0, own // requests, -1)
    before = slot[None, :] < slot[:, None]
    rank = jnp.sum((home[None, :] == home[:, None]) & before, axis=1, dtype=jnp.int32)
    place = jnp.where(own >= 0, home * CAP + rank, me * CAP)
    lent_info = jnp.concatenate([place, jnp.where(own >= 0, length, 0)])
    place_info = listed(
        picks >= 0, [jnp.arange(lend_count * CAP, dtype=jnp.int32), picks]
    )
    home_lengths = lax.dynamic_slice_in_dim(lengths, me * requests, requests)

    starts = jnp.maximum(picks, 0)
    starts = (starts // per_source) * packed_rows + (starts % per_source) * rows
    asked = pl.pallas_call(
        lambda *refs: pick_kernel(*refs, rows=rows),
        out_shape=jax.ShapeDtypeStruct((lend_count, CAP * rows, dim), jnp.bfloat16),
        in_specs=[spec(SMEM), spec(VMEM)],
        out_specs=spec(VMEM),
        compiler_params=params(8),
        name="pick",
    )(starts, packed.reshape(tp_count * packed_rows, dim))
    arrived = lax.all_to_all(asked, "lend", split_axis=0, concat_axis=0, tiled=True)

    home_out, home_lse = pl.pallas_call(
        lambda *refs: home_kernel(*refs, rows=rows, per_source=per_source),
        out_shape=[
            jax.ShapeDtypeStruct((requests, rows, dim), jnp.float32),
            jax.ShapeDtypeStruct((requests, CAP * rows), jnp.float32),
        ],
        in_specs=[spec(SMEM)] + [spec(VMEM)] * 4 + [spec(HBM)],
        out_specs=[spec(VMEM)] * 2,
        scratch_shapes=[pltpu.VMEM((rows, LANES), jnp.float32)],
        compiler_params=params(24),
        cost_estimate=pl.CostEstimate(
            flops=4 * requests * rows * HOME_CAP * dim,
            bytes_accessed=6 << 20,
            transcendentals=requests * rows * HOME_CAP,
        ),
        name="home",
    )(
        home_lengths,
        packed,
        home_keys.reshape(requests, HOME_CAP, dim),
        home_values.reshape(requests, HOME_CAP, dim),
        picks_wide,
        asked,
    )

    back = pl.pallas_call(
        lambda *refs: lent_kernel(*refs, rows=rows),
        out_shape=jax.ShapeDtypeStruct((lend_count, CAP * rows + STAT_ROWS, dim), jnp.bfloat16),
        in_specs=[spec(SMEM)] + [spec(HBM)] * 4,
        out_specs=spec(VMEM),
        scratch_shapes=[
            pltpu.VMEM((lend_count, CAP * rows, dim), jnp.bfloat16),
            pltpu.VMEM((slots, BLOCK, dim), jnp.bfloat16),
            pltpu.VMEM((slots, BLOCK, dim), jnp.bfloat16),
            pltpu.VMEM((CAP * rows, LANES), jnp.float32),
            pltpu.SemaphoreType.DMA((max(slots // LENT_GROUP, 1) + 1, 2)),
        ],
        compiler_params=params(LENT_MIB),
        name="lent",
    )(
        lent_info,
        arrived,
        lent_keys.reshape(slots, BLOCK, dim),
        lent_values.reshape(slots, BLOCK, dim),
        home_lse,
    )
    back = lax.all_to_all(back, "lend", split_axis=0, concat_axis=0, tiled=True)

    attended = pl.pallas_call(
        lambda *refs: combine_kernel(*refs, rows=rows),
        out_shape=jax.ShapeDtypeStruct((tp_count, per_source * rows, dim), jnp.bfloat16),
        in_specs=[spec(SMEM)] + [spec(VMEM)] * 4,
        out_specs=spec(VMEM),
        scratch_shapes=[
            pltpu.VMEM((requests, rows, dim), jnp.float32),
            pltpu.VMEM((lend_count, CAP * rows, LANES), jnp.float32),
        ],
        compiler_params=params(12),
        name="combine",
    )(place_info, picks_wide, back, home_out, home_lse)
    attended = lax.all_to_all(attended, "tp", split_axis=0, concat_axis=0, tiled=True)
    return jnp.swapaxes(attended.reshape(heads, per_source, rows, dim), 0, 1)


def solution(mesh):
    return jax.shard_map(
        shards,
        mesh=mesh,
        in_specs=(
            P(("lend", "tp"), None, None, None),
            P(("lend", "tp"), None, None, None),
            P(("lend", "tp"), None, None, None),
            P("lend", None, "tp", None),
            P("lend", None, "tp", None),
            P("lend", None, "tp", None),
            P("lend", None, "tp", None),
            P(),
            P(),
        ),
        out_specs=P(("lend", "tp"), None, None, None),
        check_vma=False,
    )
```

time: 236 us -> 109 us (0.46)
  waiting for transfers between devices: 133 us -> 49.1 us
  local copies, waits for them, and re-layouts: 20.2 us -> 3.54 us
  Pallas kernels: 0 us -> 15 us
  between operations: 13.7 us -> 0.13 us
  blocking collectives: 26.4 us -> 13.2 us
  matrix products: 10.3 us -> 0 us
  other arithmetic: 10.2 us -> 3.91 us
  starting transfers between devices: 20 us -> 23.8 us
    all_gather x1 -> x0, waiting for transfers between devices: 87.4 us -> none  [shards(): gathered = lax.all_gather(queries_home, 'lend', axis=0, tiled=True)]
    pallas_call x0 -> x5, Pallas kernels: none -> 15 us  [the longest x1 6.73 us: shards(): pl.pallas_call(lambda *refs: lent_kernel(*refs, rows=rows), out_shape=jax...]
    all_to_all x2 -> x1, blocking collectives: 26.4 us -> 13.2 us  [shards(): lax.all_to_all(attended, 'tp', split_axis=0, concat_axis=0, tiled=True)]
    dot_general x7 -> x0, matrix products: 10.3 us -> none  [the longest x1 3.93 us: lent_part(): jnp.einsum('skqd,sjkd->skqj', slot_queries, lent_keys, preferred_element_...]
    gather x4 -> x0, local copies, waits for them, and re-layouts: 8 us -> none  [the longest x1 4.03 us: shards(): slot_queries = jnp.take(gathered, jnp.maximum(own_owner, 0), axis=0)]
    all_to_all x3 -> x0, local copies, waits for them, and re-layouts: 4.59 us -> none  [the longest x2 3.87 us: shards(): lax.all_to_all((placed_out.reshape((lend_count, CAP) + placed_out.shape[1...]
    all_to_all x4 -> x3, starting transfers between devices: 20 us -> 23.8 us  [the longest x1 10.6 us: shards(): lax.all_to_all(asked, 'lend', split_axis=0, concat_axis=0, tiled=True)]
    unnamed x19 -> x12, local copies, waits for them, and re-layouts: 6.03 us -> 2.22 us
  transfers between devices with their start and end apart: 5 -> 3, of which waited for: 4 -> 3; matrix products, arithmetic and copies ran while one was open for 13% -> 4% of each run, Pallas kernels for 0% -> 3%
where the time goes in v1:
time: 109 us
  waiting for transfers between devices  49.1 us (45%)
  starting transfers between devices  23.8 us (22%)
  Pallas kernels  15 us (14%)
  blocking collectives  13.2 us (12%)
  other arithmetic  3.91 us (4%)
  local copies, waits for them, and re-layouts  3.54 us (3%)
    all_to_all x1, waiting for transfers between devices, shards(): back = lax.all_to_all(back, 'lend', split_axis=0, concat_axis=0, tiled=True)  25.3 us
    all_to_all x1, waiting for transfers between devices, shards(): lax.all_to_all(asked, 'lend', split_axis=0, concat_axis=0, tiled=True)  19 us
    all_to_all x1, blocking collectives, shards(): lax.all_to_all(attended, 'tp', split_axis=0, concat_axis=0, tiled=True)  13.2 us
    all_to_all x1, starting transfers between devices, shards(): lax.all_to_all(asked, 'lend', split_axis=0, concat_axis=0, tiled=True)  10.6 us
    pallas_call x1, Pallas kernels, shards(): pl.pallas_call(lambda *refs: lent_kernel(*refs, rows=rows), out_shape=jax...  6.73 us
    all_to_all x1, starting transfers between devices, shards(): lax.all_to_all(packed, 'tp', split_axis=0, concat_axis=0, tiled=True)  6.71 us
    all_to_all x1, starting transfers between devices, shards(): back = lax.all_to_all(back, 'lend', split_axis=0, concat_axis=0, tiled=True)  6.52 us
    all_to_all x1, waiting for transfers between devices, shards(): lax.all_to_all(packed, 'tp', split_axis=0, concat_axis=0, tiled=True)  4.83 us
  transfers between devices with their start and end apart: 3, of which 3 were waited for; matrix products, arithmetic and copies ran while one was open for 4% of the time, Pallas kernels for 3%

profile of v1, /device:TPU:1, one launch (start us, length us, event | category | flops | bytes accessed | tf_op | source)
XLA Modules:
  0.0 108.7 jit_solution(16270316210399673422)
XLA Ops:
  0.0 1.7 %pack.1 = bf16[8,144,128]{2,1,0:T(8,128)(2,1)} custom-call(bf16[2,8,64,128]{3,2,1,0:T(8,128)(2,1)} %queries.1, bf16[2,8,4,128]{3,2,1,0:T(4,128)(2,1)} %new_keys.1, bf16[2,8,4,128]{3,2,1,0:T(4,128)(2,1)} %new_values.1), custom_call_target="tpu_custom_call" | custom-call | tf_op jit(solution)/shard_map/pack/pallas_call | solution.py:319
  1.7 0.0 copy-start.5
  1.8 0.0 copy-start.4
  1.8 0.0 copy-start
  1.8 6.7 %all-to-all-start = ((bf16[8,144,128]{2,1,0:T(8,128)(2,1)}), bf16[8,144,128]{2,1,0:T(8,128)(2,1)S(1)}, u32[]{:S(2)}, u32[]{:S(2)}) async-start(bf16[8,144,128]{2,1,0:T(8,128)(2,1)} %pack.1), calls=%async_computation | async-start | bytes 589824 | tf_op jit(solution)/shard_map/all_to_all | solution.py:331
  8.5 0.7 broadcast_subtract_fusion
  9.2 0.1 sub.29
  9.3 0.1 fusion.5
  9.4 0.2 fusion.3
  9.6 0.7 fusion.6
  10.3 0.1 copy.16
  10.4 0.1 stack.14
  10.5 4.8 %all-to-all-done.refs_1_ = bf16[8,144,128]{2,1,0:T(8,128)(2,1)S(1)} async-done(((bf16[8,144,128]{2,1,0:T(8,128)(2,1)}), bf16[8,144,128]{2,1,0:T(8,128)(2,1)S(1)}, u32[]{:S(2)}, u32[]{:S(2)}) %all-to-all-start) | async-done | bytes 294944 | tf_op jit(solution)/shard_map/all_to_all | solution.py:331
  15.3 1.6 %pick.1.refs_5_ = bf16[32,128,128]{2,1,0:T(8,128)(2,1)} custom-call(s32[64]{0:T(128)S(1)} %get-tuple-element.11.refs_0_, bf16[1152,128]{1,0:T(8,128)(2,1)S(1)} %bitcast.12), custom_call_target="tpu_custom_call" | custom-call | tf_op jit(solution)/shard_map/pick/pallas_call | solution.py:370
  16.9 10.6 %all-to-all-start.1 = ((bf16[32,128,128]{2,1,0:T(8,128)(2,1)}), bf16[32,128,128]{2,1,0:T(8,128)(2,1)}, u32[]{:S(2)}, u32[]{:S(2)}) async-start(bf16[32,128,128]{2,1,0:T(8,128)(2,1)} %pick.1.refs_5_), calls=%async_computation.1 | async-start | bytes 2097152 | tf_op jit(solution)/shard_map/all_to_all | solution.py:378
  27.5 0.1 copy.17
  27.6 0.1 broadcast_in_dim.74
  27.7 0.1 reshape.82.refs_4_.refs_1_
  27.8 0.0 copy-done.5
  27.8 0.1 dynamic_slice.7.refs_0_
  27.8 0.0 copy-done.4
  27.8 0.1 fusion.11
  27.9 0.2 convert_reduce_fusion.2
  28.1 0.2 select_reduce_fusion
  28.3 0.2 convert_reduce_fusion
  28.5 0.6 pad_add_fusion.2.refs_0_
  29.1 0.0 copy-done
  29.1 0.0 copy-start.1
  29.1 1.6 %copy-done.1 = bf16[16,512,1,128]{3,1,2,0:T(8,128)(2,1)S(1)} copy-done((bf16[16,512,1,128]{3,1,2,0:T(8,128)(2,1)S(1)}, bf16[16,512,1,128]{3,1,2,0:T(8,128)(2,1)}, u32[]{:S(2)}) %copy-start.1) | copy-done | bytes 2097176
  30.7 2.9 %home.1 = (f32[16,64,128]{2,1,0:T(8,128)S(1)}, f32[16,128]{1,0:T(8,128)S(1)}) custom-call(s32[16]{0:T(128)S(1)} %dynamic_slice.7.refs_0_, bf16[8,144,128]{2,1,0:T(8,128)(2,1)S(1)} %all-to-all-done.refs_1_, bf16[16,512,128]{2,1,0:T(8,128)(2,1)S(1)} %bitcast.13, bf16[16,512,128]{2,1,0:T(8,128)(2,1)S(1)} %bitcast.14, s32[32,128]{1,0:T(8,128)S(1)} %reshape.82.refs_4_.refs_1_, ...), custom_call_target="tpu_custom_call" | custom-call | flops 268435456 | bytes 6291456 | tf_op jit(solution)/shard_map/home/pallas_call | solution.py:380
  33.6 0.0 copy-start.2
  33.6 0.6 copy-done.2
  34.2 19.0 %all-to-all-done.1.refs_1_ = bf16[32,128,128]{2,1,0:T(8,128)(2,1)} async-done(((bf16[32,128,128]{2,1,0:T(8,128)(2,1)}), bf16[32,128,128]{2,1,0:T(8,128)(2,1)}, u32[]{:S(2)}, u32[]{:S(2)}) %all-to-all-start.1) | async-done | bytes 1048608 | tf_op jit(solution)/shard_map/all_to_all | solution.py:378
  53.3 6.7 %lent.1 = bf16[32,136,128]{2,1,0:T(8,128)(2,1)} custom-call(s32[64]{0:T(128)} %pad_add_fusion.2.refs_0_, bf16[32,128,128]{2,1,0:T(8,128)(2,1)} %all-to-all-done.1.refs_1_, bf16[32,512,128]{2,1,0:T(8,128)(2,1)} %bitcast.15, bf16[32,512,128]{2,1,0:T(8,128)(2,1)} %bitcast.16, f32[16,128]{1,0:T(8,128)} %copy-done.2), custom_call_target="tpu_custom_call" | custom-call | tf_op jit(solution)/shard_map/lent/pallas_call | solution.py:405
  60.0 0.0 copy-start.3
  60.0 6.5 %all-to-all-start.2 = ((bf16[32,136,128]{2,1,0:T(8,128)(2,1)}), bf16[32,136,128]{2,1,0:T(8,128)(2,1)S(1)}, u32[]{:S(2)}, u32[]{:S(2)}) async-start(bf16[32,136,128]{2,1,0:T(8,128)(2,1)} %lent.1), calls=%async_computation.2 | async-start | bytes 2228224 | tf_op jit(solution)/shard_map/all_to_all | solution.py:426
  66.5 0.1 convert_reduce_fusion.1
  66.7 0.1 select_reduce_fusion.2
  66.8 0.7 pad_add_fusion.1.refs_0_
  67.5 25.3 %all-to-all-done.2.refs_2_ = bf16[32,136,128]{2,1,0:T(8,128)(2,1)S(1)} async-done(((bf16[32,136,128]{2,1,0:T(8,128)(2,1)}), bf16[32,136,128]{2,1,0:T(8,128)(2,1)S(1)}, u32[]{:S(2)}, u32[]{:S(2)}) %all-to-all-start.2) | async-done | bytes 1114144 | tf_op jit(solution)/shard_map/all_to_all | solution.py:426
  92.8 0.0 copy-done.3
  92.8 2.0 %combine.1 = bf16[8,128,128]{2,1,0:T(8,128)(2,1)S(1)} custom-call(s32[129]{0:T(256)S(1)} %pad_add_fusion.1.refs_0_, s32[32,128]{1,0:T(8,128)S(1)} %reshape.82.refs_4_.refs_1_, bf16[32,136,128]{2,1,0:T(8,128)(2,1)S(1)} %all-to-all-done.2.refs_2_, f32[16,64,128]{2,1,0:T(8,128)S(1)} %get-tuple-element.8.refs_3_, f32[16,128]{1,0:T(8,128)S(1)} %copy-done.3), custom_call_target="tpu_custom_call" | custom-call | tf_op jit(solution)/shard_map/combine/pallas_call | solution.py:428
  94.8 13.2 %all_to_all.20 = bf16[8,128,128]{2,1,0:T(8,128)(2,1)S(1)} all-to-all(bf16[8,128,128]{2,1,0:T(8,128)(2,1)S(1)} %combine.1), channel_id=1, replica_groups=mesh['lend'=32,'tp'=8] {'tp'}, dimensions={0} | all-to-all | bytes 524288 | tf_op jit(solution)/shard_map/all_to_all | solution.py:440
  108.0 0.7 copy.20
  (4 shorter events, 0.0 us)
Async XLA Ops:
  1.7 26.0 %copy-start.5 = (s32[512]{0:T(512)S(1)}, s32[512]{0:T(512)}, u32[]{:S(2)}) copy-start(s32[512]{0:T(512)} %param.16) | copy-start | bytes 6148
  1.8 26.1 %copy-start.4 = (s32[1024]{0:T(1024)S(1)}, s32[1024]{0:T(1024)}, u32[]{:S(2)}) copy-start(s32[1024]{0:T(1024)} %param.17) | copy-start | bytes 12292
  1.8 27.3 %copy-start = (bf16[16,512,1,128]{3,1,2,0:T(8,128)(2,1)S(1)}, bf16[16,512,1,128]{3,1,2,0:T(8,128)(2,1)}, u32[]{:S(2)}) copy-start(bf16[16,512,1,128]{3,1,2,0:T(8,128)(2,1)} %param.12) | copy-start | bytes 6291460
  1.8 13.5 %all-to-all-start = ((bf16[8,144,128]{2,1,0:T(8,128)(2,1)}), bf16[8,144,128]{2,1,0:T(8,128)(2,1)S(1)}, u32[]{:S(2)}, u32[]{:S(2)}) async-start(bf16[8,144,128]{2,1,0:T(8,128)(2,1)} %pack.1), calls=%async_computation | async-start | bytes 589824 | tf_op jit(solution)/shard_map/all_to_all | solution.py:331
  16.9 36.3 %all-to-all-start.1 = ((bf16[32,128,128]{2,1,0:T(8,128)(2,1)}), bf16[32,128,128]{2,1,0:T(8,128)(2,1)}, u32[]{:S(2)}, u32[]{:S(2)}) async-start(bf16[32,128,128]{2,1,0:T(8,128)(2,1)} %pick.1.refs_5_), calls=%async_computation.1 | async-start | bytes 2097152 | tf_op jit(solution)/shard_map/all_to_all | solution.py:378
  29.1 1.6 %copy-start.1 = (bf16[16,512,1,128]{3,1,2,0:T(8,128)(2,1)S(1)}, bf16[16,512,1,128]{3,1,2,0:T(8,128)(2,1)}, u32[]{:S(2)}) copy-start(bf16[16,512,1,128]{3,1,2,0:T(8,128)(2,1)} %param.13) | copy-start | bytes 6291460
  33.6 0.6 copy-start.2
  60.0 32.8 %copy-start.3 = (f32[16,128]{1,0:T(8,128)S(1)}, f32[16,128]{1,0:T(8,128)}, u32[]{:S(2)}) copy-start(f32[16,128]{1,0:T(8,128)} %copy-done.2) | copy-start | bytes 24580
  60.0 32.8 %all-to-all-start.2 = ((bf16[32,136,128]{2,1,0:T(8,128)(2,1)}), bf16[32,136,128]{2,1,0:T(8,128)(2,1)S(1)}, u32[]{:S(2)}, u32[]{:S(2)}) async-start(bf16[32,136,128]{2,1,0:T(8,128)(2,1)} %lent.1), calls=%async_computation.2 | async-start | bytes 2228224 | tf_op jit(solution)/shard_map/all_to_all | solution.py:426

commit v2 on v1

--- a/solution.py
+++ b/solution.py
@@ -59,19 +59,31 @@
         copy.start()
     for copy in fresh:
         copy.wait()
+    fresh = [news[kind].astype(jnp.float32) for kind in range(2)]
     for head in range(heads):
-        block = [news[kind, part, head] for kind in range(2) for part in range(per_source)]
-        block = jnp.concatenate([array.astype(jnp.float32) for array in block], axis=0)
+        starts = [(part * heads + head) * STEPS for part in range(per_source)]
+        block = [array[start : start + STEPS] for array in fresh for start in starts]
+        block = jnp.concatenate(block, axis=0)
         out[head, per_source * rows :, :] = block.astype(jnp.bfloat16)
     for copy in copies:
         copy.wait()
 
 
-def pick_kernel(starts, packed_ref, out_ref, *, rows):
-    for place in range(out_ref.shape[0] * CAP):
-        lender, rank = divmod(place, CAP)
-        start = pl.multiple_of(starts[place], 16)
-        out_ref[lender, rank * rows : (rank + 1) * rows, :] = packed_ref[pl.ds(start, rows), :]
+def pick_kernel(starts, packed_ref, out_hbm, picked, sems, *, rows):
+    lenders = picked.shape[0]
+    parts = sems.shape[0]
+    size = lenders // parts
+    copies = []
+    for part in range(parts):
+        for place in range(part * size * CAP, (part + 1) * size * CAP):
+            lender, rank = divmod(place, CAP)
+            start = pl.multiple_of(starts[place], 16)
+            picked[lender, rank * rows : (rank + 1) * rows, :] = packed_ref[pl.ds(start, rows), :]
+        span = slice(part * size, (part + 1) * size)
+        copies.append(pltpu.make_async_copy(picked.at[span], out_hbm.at[span], sems.at[part]))
+        copies[-1].start()
+    for copy in copies:
+        copy.wait()
 
 
 def home_kernel(
@@ -139,46 +151,52 @@
 
 
 def lent_kernel(
-    info,
+    info_hbm,
     query_hbm,
     keys_hbm,
     values_hbm,
     home_lse,
     out_ref,
+    info,
     queries,
     keys,
     values,
     stats,
     sems,
+    ends,
     *,
     rows,
+    chunks,
 ):
     slots = keys_hbm.shape[0]
     homes = query_hbm.shape[0]
-    group = min(LENT_GROUP, slots)
-    chunks = slots // group
     factor = 1.0 / math.sqrt(query_hbm.shape[-1])
 
-    def copy(kind, chunk):
-        source, target = ((keys_hbm, keys), (values_hbm, values))[kind]
-        part = pl.ds(chunk * group, group)
-        return pltpu.make_async_copy(source.at[part], target.at[part], sems.at[chunk, kind])
-
-    arrival = pltpu.make_async_copy(query_hbm, queries, sems.at[chunks, 0])
-    arrival.start()
-    for chunk in range(chunks):
-        for kind in range(2):
-            copy(kind, chunk).start()
+    def copies(chunk):
+        first, size = chunks[chunk]
+        span = slice(first, first + size)
+        return [
+            pltpu.make_async_copy(source.at[span], target.at[span], sems.at[chunk, kind])
+            for kind, (source, target) in enumerate(((keys_hbm, keys), (values_hbm, values)))
+        ]
+
+    arrivals = [
+        pltpu.make_async_copy(info_hbm, info, ends.at[0]),
+        pltpu.make_async_copy(query_hbm, queries, ends.at[1]),
+    ]
+    pending = [copies(chunk) for chunk in range(len(chunks))]
+    for copy in arrivals + [copy for pair in pending for copy in pair]:
+        copy.start()
     stats[...] = jnp.zeros_like(stats)
     lane = lax.broadcasted_iota(jnp.int32, (rows, stats.shape[1]), 1)
-    arrival.wait()
-
-    def some(chunk, carry):
-        for kind in range(2):
-            copy(kind, chunk).wait()
+    for copy in arrivals:
+        copy.wait()
+
+    for (first, size), pair in zip(chunks, pending):
+        for copy in pair:
+            copy.wait()
         scores, placed, mixed, total = [], [], [], []
-        for near in range(group):
-            slot = chunk * group + near
+        for slot in range(first, first + size):
             place = info[slot]
             length = info[slots + slot]
             home = lax.div(place, CAP)
@@ -188,10 +206,10 @@
             scores.append(jnp.where(position < length, raw, NEG_BIG))
             placed.append((home, start))
         tops = [jnp.max(old, axis=1, keepdims=True) for old in scores]
-        for near in range(group):
+        for near in range(size):
             terms = jnp.exp2((scores[near] - tops[near]) * (factor * LOG2E))
             total.append(jnp.sum(terms, axis=1, keepdims=True))
-            mixed.append(nn_dot(terms.astype(jnp.bfloat16), values[chunk * group + near]))
+            mixed.append(nn_dot(terms.astype(jnp.bfloat16), values[first + near]))
         for near, (home, start) in enumerate(placed):
             out_ref[home, pl.ds(start, rows), :] = (mixed[near] * (1.0 / total[near])).astype(
                 jnp.bfloat16
@@ -201,9 +219,7 @@
                 tops[near] * factor + jnp.log(total[near]),
                 stats[pl.ds(start, rows), :],
             )
-        return carry
-
-    lax.fori_loop(0, chunks, some, 0)
+
     turned = stats[...].T[:homes]
     high = turned.astype(jnp.bfloat16).astype(jnp.float32)
     middle = (turned - high).astype(jnp.bfloat16).astype(jnp.float32)
@@ -219,12 +235,14 @@
 
 
 def combine_kernel(
-    info, picks_wide, back_ref, home_out, home_lse, out_ref, mixed, wide, *, rows
+    info_hbm, picks_wide, back_ref, home_out, home_lse, out_ref, info, mixed, wide, sem, *, rows
 ):
     lenders = back_ref.shape[0]
     requests = home_out.shape[0]
     count = out_ref.shape[0]
     per_target = requests // count
+    arrival = pltpu.make_async_copy(info_hbm, info, sem)
+    arrival.start()
 
     lse = jnp.sum(back_ref[:, CAP * rows :, :].astype(jnp.float32), axis=1)
     owner = picks_wide[...]
@@ -258,6 +276,7 @@
 
     for request in range(requests):
         mixed[request] = home_out[request] * home_turned[:rows, request : request + 1]
+    arrival.wait()
     filled = info[0]
     places = lenders * CAP
 
@@ -281,6 +300,10 @@
             out_ref[target, part * rows : (part + 1) * rows, :] = mixed[
                 target * per_target + part
             ].astype(jnp.bfloat16)
+
+
+def padded(table):
+    return jnp.pad(table, (0, -table.shape[0] % LANES))
 
 
 def listed(present, columns):
@@ -322,12 +345,12 @@
         in_specs=[spec(HBM)] * 3,
         out_specs=spec(VMEM),
         scratch_shapes=[
-            pltpu.VMEM((2,) + new_keys.shape, jnp.bfloat16),
+            pltpu.VMEM((2, per_source * heads * STEPS, dim), jnp.bfloat16),
             pltpu.SemaphoreType.DMA((2 + per_source,)),
         ],
         compiler_params=params(60),
         name="pack",
-    )(queries, new_keys, new_values)
+    )(queries, new_keys.reshape(-1, dim), new_values.reshape(-1, dim))
     packed = lax.all_to_all(packed, "tp", split_axis=0, concat_axis=0, tiled=True)
 
     table = slot_owner.reshape(lend_count, slots)
@@ -359,9 +382,9 @@
     before = slot[None, :] < slot[:, None]
     rank = jnp.sum((home[None, :] == home[:, None]) & before, axis=1, dtype=jnp.int32)
     place = jnp.where(own >= 0, home * CAP + rank, me * CAP)
-    lent_info = jnp.concatenate([place, jnp.where(own >= 0, length, 0)])
-    place_info = listed(
-        picks >= 0, [jnp.arange(lend_count * CAP, dtype=jnp.int32), picks]
+    lent_info = padded(jnp.concatenate([place, jnp.where(own >= 0, length, 0)]))
+    place_info = padded(
+        listed(picks >= 0, [jnp.arange(lend_count * CAP, dtype=jnp.int32), picks])
     )
     home_lengths = lax.dynamic_slice_in_dim(lengths, me * requests, requests)
 
@@ -371,7 +394,11 @@
         lambda *refs: pick_kernel(*refs, rows=rows),
         out_shape=jax.ShapeDtypeStruct((lend_count, CAP * rows, dim), jnp.bfloat16),
         in_specs=[spec(SMEM), spec(VMEM)],
-        out_specs=spec(VMEM),
+        out_specs=spec(HBM),
+        scratch_shapes=[
+            pltpu.VMEM((lend_count, CAP * rows, dim), jnp.bfloat16),
+            pltpu.SemaphoreType.DMA((4,)),
+        ],
         compiler_params=params(8),
         name="pick",
     )(starts, packed.reshape(tp_count * packed_rows, dim))
@@ -402,17 +429,22 @@
         asked,
     )
 
+    sizes = [LENT_GROUP // 2] * 2 + [LENT_GROUP] * (slots // LENT_GROUP - 1)
+    chunks = [(sum(sizes[:index]), size) for index, size in enumerate(sizes)]
+    back_shape = (lend_count, CAP * rows + STAT_ROWS, dim)
     back = pl.pallas_call(
-        lambda *refs: lent_kernel(*refs, rows=rows),
-        out_shape=jax.ShapeDtypeStruct((lend_count, CAP * rows + STAT_ROWS, dim), jnp.bfloat16),
-        in_specs=[spec(SMEM)] + [spec(HBM)] * 4,
+        lambda *refs: lent_kernel(*refs, rows=rows, chunks=chunks),
+        out_shape=jax.ShapeDtypeStruct(back_shape, jnp.bfloat16),
+        in_specs=[spec(HBM)] * 5,
         out_specs=spec(VMEM),
         scratch_shapes=[
+            pltpu.SMEM(lent_info.shape, jnp.int32),
             pltpu.VMEM((lend_count, CAP * rows, dim), jnp.bfloat16),
             pltpu.VMEM((slots, BLOCK, dim), jnp.bfloat16),
             pltpu.VMEM((slots, BLOCK, dim), jnp.bfloat16),
             pltpu.VMEM((CAP * rows, LANES), jnp.float32),
-            pltpu.SemaphoreType.DMA((max(slots // LENT_GROUP, 1) + 1, 2)),
+            pltpu.SemaphoreType.DMA((len(chunks), 2)),
+            pltpu.SemaphoreType.DMA((2,)),
         ],
         compiler_params=params(LENT_MIB),
         name="lent",
@@ -428,11 +460,13 @@
     attended = pl.pallas_call(
         lambda *refs: combine_kernel(*refs, rows=rows),
         out_shape=jax.ShapeDtypeStruct((tp_count, per_source * rows, dim), jnp.bfloat16),
-        in_specs=[spec(SMEM)] + [spec(VMEM)] * 4,
+        in_specs=[spec(HBM)] + [spec(VMEM)] * 4,
         out_specs=spec(VMEM),
         scratch_shapes=[
+            pltpu.SMEM(place_info.shape, jnp.int32),
             pltpu.VMEM((requests, rows, dim), jnp.float32),
             pltpu.VMEM((lend_count, CAP * rows, LANES), jnp.float32),
+            pltpu.SemaphoreType.DMA,
         ],
         compiler_params=params(12),
         name="combine",

time: 109 us -> 110 us (level)
    pallas_call x1, Pallas kernels: 6.73 us -> 8.04 us  [shards(): pl.pallas_call(lambda *refs: lent_kernel(*refs, rows=rows, chunks=chunks)...]
where the time goes in v2:
time: 110 us
  waiting for transfers between devices  49.1 us (45%)
  starting transfers between devices  23.8 us (22%)
  Pallas kernels  15.9 us (14%)
  blocking collectives  13.2 us (12%)
  local copies, waits for them, and re-layouts  4.08 us (4%)
  other arithmetic  3.39 us (3%)
    all_to_all x1, waiting for transfers between devices, shards(): back = lax.all_to_all(back, 'lend', split_axis=0, concat_axis=0, tiled=True)  25.3 us
    all_to_all x1, waiting for transfers between devices, shards(): lax.all_to_all(asked, 'lend', split_axis=0, concat_axis=0, tiled=True)  19 us
    all_to_all x1, blocking collectives, shards(): lax.all_to_all(attended, 'tp', split_axis=0, concat_axis=0, tiled=True)  13.2 us
    all_to_all x1, starting transfers between devices, shards(): lax.all_to_all(asked, 'lend', split_axis=0, concat_axis=0, tiled=True)  10.6 us
    pallas_call x1, Pallas kernels, shards(): pl.pallas_call(lambda *refs: lent_kernel(*refs, rows=rows, chunks=chunks)...  8.04 us
    all_to_all x1, starting transfers between devices, shards(): lax.all_to_all(packed, 'tp', split_axis=0, concat_axis=0, tiled=True)  6.71 us
    all_to_all x1, starting transfers between devices, shards(): back = lax.all_to_all(back, 'lend', split_axis=0, concat_axis=0, tiled=True)  6.51 us
    all_to_all x1, waiting for transfers between devices, shards(): lax.all_to_all(packed, 'tp', split_axis=0, concat_axis=0, tiled=True)  4.83 us
  transfers between devices with their start and end apart: 3, of which 3 were waited for; matrix products, arithmetic and copies ran while one was open for 4% of the time, Pallas kernels for 3%

profile of v2, /device:TPU:1, one launch (start us, length us, event | category | flops | bytes accessed | tf_op | source)
XLA Modules:
  0.0 109.6 jit_solution(7451765569878739820)
XLA Ops:
  0.0 1.7 %pack.1 = bf16[8,144,128]{2,1,0:T(8,128)(2,1)} custom-call(bf16[2,8,64,128]{3,2,1,0:T(8,128)(2,1)} %queries.1, bf16[64,128]{1,0:T(8,128)(2,1)} %bitcast.20, bf16[64,128]{1,0:T(8,128)(2,1)} %bitcast.21), custom_call_target="tpu_custom_call" | custom-call | tf_op jit(solution)/shard_map/pack/pallas_call | solution.py:342
  1.7 0.0 copy-start.4
  1.8 0.0 copy-start.5
  1.8 0.0 copy-start
  1.8 6.7 %all-to-all-start = ((bf16[8,144,128]{2,1,0:T(8,128)(2,1)}), bf16[8,144,128]{2,1,0:T(8,128)(2,1)S(1)}, u32[]{:S(2)}, u32[]{:S(2)}) async-start(bf16[8,144,128]{2,1,0:T(8,128)(2,1)} %pack.1), calls=%async_computation | async-start | bytes 589824 | tf_op jit(solution)/shard_map/all_to_all | solution.py:354
  8.5 0.7 broadcast_subtract_fusion
  9.2 0.1 sub.29
  9.3 0.1 fusion.5
  9.4 0.2 fusion.3
  9.6 0.7 fusion.6
  10.3 0.1 copy.16
  10.4 0.1 stack.14
  10.5 4.8 %all-to-all-done.refs_1_ = bf16[8,144,128]{2,1,0:T(8,128)(2,1)S(1)} async-done(((bf16[8,144,128]{2,1,0:T(8,128)(2,1)}), bf16[8,144,128]{2,1,0:T(8,128)(2,1)S(1)}, u32[]{:S(2)}, u32[]{:S(2)}) %all-to-all-start) | async-done | bytes 294944 | tf_op jit(solution)/shard_map/all_to_all | solution.py:354
  15.3 1.6 %pick.1.refs_5_ = bf16[32,128,128]{2,1,0:T(8,128)(2,1)} custom-call(s32[64]{0:T(128)S(1)} %get-tuple-element.11.refs_0_, bf16[1152,128]{1,0:T(8,128)(2,1)S(1)} %bitcast.14), custom_call_target="tpu_custom_call" | custom-call | tf_op jit(solution)/shard_map/pick/pallas_call | solution.py:393
  16.9 10.6 %all-to-all-start.1 = ((bf16[32,128,128]{2,1,0:T(8,128)(2,1)}), bf16[32,128,128]{2,1,0:T(8,128)(2,1)}, u32[]{:S(2)}, u32[]{:S(2)}) async-start(bf16[32,128,128]{2,1,0:T(8,128)(2,1)} %pick.1.refs_5_), calls=%async_computation.1 | async-start | bytes 2097152 | tf_op jit(solution)/shard_map/all_to_all | solution.py:405
  27.5 0.0 copy-done.4
  27.5 0.1 fusion.11
  27.6 0.2 convert_reduce_fusion.2
  27.8 0.0 copy-done.5
  27.8 0.2 select_reduce_fusion
  28.0 0.2 convert_reduce_fusion
  28.2 0.1 pad_add_fusion.2
  28.3 0.5 pad.9.refs_0_
  28.8 0.1 copy.17
  28.9 0.1 broadcast_in_dim.74
  29.0 0.1 reshape.88.refs_4_.refs_1_
  29.0 0.1 dynamic_slice.7.refs_0_
  29.1 0.0 copy-done
  29.1 0.0 copy-start.1
  29.1 1.6 %copy-done.1 = bf16[16,512,1,128]{3,1,2,0:T(8,128)(2,1)S(1)} copy-done((bf16[16,512,1,128]{3,1,2,0:T(8,128)(2,1)S(1)}, bf16[16,512,1,128]{3,1,2,0:T(8,128)(2,1)}, u32[]{:S(2)}) %copy-start.1) | copy-done | bytes 2097176
  30.7 2.9 %home.1 = (f32[16,64,128]{2,1,0:T(8,128)S(1)}, f32[16,128]{1,0:T(8,128)S(1)}) custom-call(s32[16]{0:T(128)S(1)} %dynamic_slice.7.refs_0_, bf16[8,144,128]{2,1,0:T(8,128)(2,1)S(1)} %all-to-all-done.refs_1_, bf16[16,512,128]{2,1,0:T(8,128)(2,1)S(1)} %bitcast.15, bf16[16,512,128]{2,1,0:T(8,128)(2,1)S(1)} %bitcast.16, s32[32,128]{1,0:T(8,128)S(1)} %reshape.88.refs_4_.refs_1_, ...), custom_call_target="tpu_custom_call" | custom-call | flops 268435456 | bytes 6291456 | tf_op jit(solution)/shard_map/home/pallas_call | solution.py:407
  33.7 0.0 copy-start.2
  33.7 0.6 copy-done.2
  34.3 19.0 %all-to-all-done.1.refs_1_ = bf16[32,128,128]{2,1,0:T(8,128)(2,1)} async-done(((bf16[32,128,128]{2,1,0:T(8,128)(2,1)}), bf16[32,128,128]{2,1,0:T(8,128)(2,1)}, u32[]{:S(2)}, u32[]{:S(2)}) %all-to-all-start.1) | async-done | bytes 1048608 | tf_op jit(solution)/shard_map/all_to_all | solution.py:405
  53.3 8.0 %lent.1 = bf16[32,136,128]{2,1,0:T(8,128)(2,1)} custom-call(s32[128]{0:T(128)} %pad.9.refs_0_, bf16[32,128,128]{2,1,0:T(8,128)(2,1)} %all-to-all-done.1.refs_1_, bf16[32,512,128]{2,1,0:T(8,128)(2,1)} %bitcast.17, bf16[32,512,128]{2,1,0:T(8,128)(2,1)} %bitcast.18, f32[16,128]{1,0:T(8,128)} %copy-done.2), custom_call_target="tpu_custom_call" | custom-call | tf_op jit(solution)/shard_map/lent/pallas_call | solution.py:435
  61.3 0.0 copy-start.3
  61.3 6.5 %all-to-all-start.2 = ((bf16[32,136,128]{2,1,0:T(8,128)(2,1)}), bf16[32,136,128]{2,1,0:T(8,128)(2,1)S(1)}, u32[]{:S(2)}, u32[]{:S(2)}) async-start(bf16[32,136,128]{2,1,0:T(8,128)(2,1)} %lent.1), calls=%async_computation.2 | async-start | bytes 2228224 | tf_op jit(solution)/shard_map/all_to_all | solution.py:458
  67.9 0.1 convert_reduce_fusion.1
  68.0 0.1 select_reduce_fusion.2
  68.1 0.7 pad_add_fusion.1
  68.8 25.3 %all-to-all-done.2.refs_2_ = bf16[32,136,128]{2,1,0:T(8,128)(2,1)S(1)} async-done(((bf16[32,136,128]{2,1,0:T(8,128)(2,1)}), bf16[32,136,128]{2,1,0:T(8,128)(2,1)S(1)}, u32[]{:S(2)}, u32[]{:S(2)}) %all-to-all-start.2) | async-done | bytes 1114144 | tf_op jit(solution)/shard_map/all_to_all | solution.py:458
  94.1 0.0 copy-done.3
  94.1 1.6 %combine.1 = bf16[8,128,128]{2,1,0:T(8,128)(2,1)S(1)} custom-call(s32[256]{0:T(256)S(1)} %pad.8.refs_0_, s32[32,128]{1,0:T(8,128)S(1)} %reshape.88.refs_4_.refs_1_, bf16[32,136,128]{2,1,0:T(8,128)(2,1)S(1)} %all-to-all-done.2.refs_2_, f32[16,64,128]{2,1,0:T(8,128)S(1)} %get-tuple-element.8.refs_3_, f32[16,128]{1,0:T(8,128)S(1)} %copy-done.3), custom_call_target="tpu_custom_call" | custom-call | tf_op jit(solution)/shard_map/combine/pallas_call | solution.py:460
  95.7 13.2 %all_to_all.20 = bf16[8,128,128]{2,1,0:T(8,128)(2,1)S(1)} all-to-all(bf16[8,128,128]{2,1,0:T(8,128)(2,1)S(1)} %combine.1), channel_id=1, replica_groups=mesh['lend'=32,'tp'=8] {'tp'}, dimensions={0} | all-to-all | bytes 524288 | tf_op jit(solution)/shard_map/all_to_all | solution.py:474
  108.9 0.7 copy.20
  (5 shorter events, 0.0 us)
Async XLA Ops:
  1.7 25.7 %copy-start.4 = (s32[1024]{0:T(1024)S(1)}, s32[1024]{0:T(1024)}, u32[]{:S(2)}) copy-start(s32[1024]{0:T(1024)} %param.17) | copy-start | bytes 12292
  1.8 26.0 %copy-start.5 = (s32[512]{0:T(512)S(1)}, s32[512]{0:T(512)}, u32[]{:S(2)}) copy-start(s32[512]{0:T(512)} %param.16) | copy-start | bytes 6148
  1.8 27.4 %copy-start = (bf16[16,512,1,128]{3,1,2,0:T(8,128)(2,1)S(1)}, bf16[16,512,1,128]{3,1,2,0:T(8,128)(2,1)}, u32[]{:S(2)}) copy-start(bf16[16,512,1,128]{3,1,2,0:T(8,128)(2,1)} %param.12) | copy-start | bytes 6291460
  1.8 13.5 %all-to-all-start = ((bf16[8,144,128]{2,1,0:T(8,128)(2,1)}), bf16[8,144,128]{2,1,0:T(8,128)(2,1)S(1)}, u32[]{:S(2)}, u32[]{:S(2)}) async-start(bf16[8,144,128]{2,1,0:T(8,128)(2,1)} %pack.1), calls=%async_computation | async-start | bytes 589824 | tf_op jit(solution)/shard_map/all_to_all | solution.py:354
  16.9 36.3 %all-to-all-start.1 = ((bf16[32,128,128]{2,1,0:T(8,128)(2,1)}), bf16[32,128,128]{2,1,0:T(8,128)(2,1)}, u32[]{:S(2)}, u32[]{:S(2)}) async-start(bf16[32,128,128]{2,1,0:T(8,128)(2,1)} %pick.1.refs_5_), calls=%async_computation.1 | async-start | bytes 2097152 | tf_op jit(solution)/shard_map/all_to_all | solution.py:405
  29.1 1.6 %copy-start.1 = (bf16[16,512,1,128]{3,1,2,0:T(8,128)(2,1)S(1)}, bf16[16,512,1,128]{3,1,2,0:T(8,128)(2,1)}, u32[]{:S(2)}) copy-start(bf16[16,512,1,128]{3,1,2,0:T(8,128)(2,1)} %param.13) | copy-start | bytes 6291460
  33.7 0.6 copy-start.2
  61.3 32.8 %copy-start.3 = (f32[16,128]{1,0:T(8,128)S(1)}, f32[16,128]{1,0:T(8,128)}, u32[]{:S(2)}) copy-start(f32[16,128]{1,0:T(8,128)} %copy-done.2) | copy-start | bytes 24580
  61.3 32.8 %all-to-all-start.2 = ((bf16[32,136,128]{2,1,0:T(8,128)(2,1)}), bf16[32,136,128]{2,1,0:T(8,128)(2,1)S(1)}, u32[]{:S(2)}, u32[]{:S(2)}) async-start(bf16[32,136,128]{2,1,0:T(8,128)(2,1)} %lent.1), calls=%async_computation.2 | async-start | bytes 2228224 | tf_op jit(solution)/shard_map/all_to_all | solution.py:458

commit v3 on v2

--- a/solution.py
+++ b/solution.py
@@ -166,37 +166,38 @@
     ends,
     *,
     rows,
-    chunks,
 ):
     slots = keys_hbm.shape[0]
     homes = query_hbm.shape[0]
+    group = min(LENT_GROUP, slots)
+    chunks = slots // group
     factor = 1.0 / math.sqrt(query_hbm.shape[-1])
 
-    def copies(chunk):
-        first, size = chunks[chunk]
-        span = slice(first, first + size)
-        return [
-            pltpu.make_async_copy(source.at[span], target.at[span], sems.at[chunk, kind])
-            for kind, (source, target) in enumerate(((keys_hbm, keys), (values_hbm, values)))
-        ]
+    def copy(kind, chunk):
+        source, target = ((keys_hbm, keys), (values_hbm, values))[kind]
+        part = pl.ds(chunk * group, group)
+        return pltpu.make_async_copy(source.at[part], target.at[part], sems.at[chunk, kind])
 
     arrivals = [
         pltpu.make_async_copy(info_hbm, info, ends.at[0]),
         pltpu.make_async_copy(query_hbm, queries, ends.at[1]),
     ]
-    pending = [copies(chunk) for chunk in range(len(chunks))]
-    for copy in arrivals + [copy for pair in pending for copy in pair]:
-        copy.start()
+    for arrival in arrivals:
+        arrival.start()
+    for chunk in range(chunks):
+        for kind in range(2):
+            copy(kind, chunk).start()
     stats[...] = jnp.zeros_like(stats)
     lane = lax.broadcasted_iota(jnp.int32, (rows, stats.shape[1]), 1)
-    for copy in arrivals:
-        copy.wait()
-
-    for (first, size), pair in zip(chunks, pending):
-        for copy in pair:
-            copy.wait()
+    for arrival in arrivals:
+        arrival.wait()
+
+    def some(chunk, carry):
+        for kind in range(2):
+            copy(kind, chunk).wait()
         scores, placed, mixed, total = [], [], [], []
-        for slot in range(first, first + size):
+        for near in range(group):
+            slot = chunk * group + near
             place = info[slot]
             length = info[slots + slot]
             home = lax.div(place, CAP)
@@ -206,10 +207,10 @@
             scores.append(jnp.where(position < length, raw, NEG_BIG))
             placed.append((home, start))
         tops = [jnp.max(old, axis=1, keepdims=True) for old in scores]
-        for near in range(size):
+        for near in range(group):
             terms = jnp.exp2((scores[near] - tops[near]) * (factor * LOG2E))
             total.append(jnp.sum(terms, axis=1, keepdims=True))
-            mixed.append(nn_dot(terms.astype(jnp.bfloat16), values[first + near]))
+            mixed.append(nn_dot(terms.astype(jnp.bfloat16), values[chunk * group + near]))
         for near, (home, start) in enumerate(placed):
             out_ref[home, pl.ds(start, rows), :] = (mixed[near] * (1.0 / total[near])).astype(
                 jnp.bfloat16
@@ -219,7 +220,9 @@
                 tops[near] * factor + jnp.log(total[near]),
                 stats[pl.ds(start, rows), :],
             )
-
+        return carry
+
+    lax.fori_loop(0, chunks, some, 0)
     turned = stats[...].T[:homes]
     high = turned.astype(jnp.bfloat16).astype(jnp.float32)
     middle = (turned - high).astype(jnp.bfloat16).astype(jnp.float32)
@@ -429,11 +432,9 @@
         asked,
     )
 
-    sizes = [LENT_GROUP // 2] * 2 + [LENT_GROUP] * (slots // LENT_GROUP - 1)
-    chunks = [(sum(sizes[:index]), size) for index, size in enumerate(sizes)]
     back_shape = (lend_count, CAP * rows + STAT_ROWS, dim)
     back = pl.pallas_call(
-        lambda *refs: lent_kernel(*refs, rows=rows, chunks=chunks),
+        lambda *refs: lent_kernel(*refs, rows=rows),
         out_shape=jax.ShapeDtypeStruct(back_shape, jnp.bfloat16),
         in_specs=[spec(HBM)] * 5,
         out_specs=spec(VMEM),
@@ -443,7 +444,7 @@
             pltpu.VMEM((slots, BLOCK, dim), jnp.bfloat16),
             pltpu.VMEM((slots, BLOCK, dim), jnp.bfloat16),
             pltpu.VMEM((CAP * rows, LANES), jnp.float32),
-            pltpu.SemaphoreType.DMA((len(chunks), 2)),
+            pltpu.SemaphoreType.DMA((max(slots // LENT_GROUP, 1), 2)),
             pltpu.SemaphoreType.DMA((2,)),
         ],
         compiler_params=params(LENT_MIB),

time: 110 us -> 110 us (level)
  no operation moved by 1% of the time
where the time goes in v3:
time: 110 us; the launch traced here: 109 us
  waiting for transfers between devices  49.2 us (45%)
  starting transfers between devices  23.8 us (22%)
  Pallas kernels  15.5 us (14%)
  blocking collectives  13.1 us (12%)
  local copies, waits for them, and re-layouts  4.08 us (4%)
  other arithmetic  3.39 us (3%)
    all_to_all x1, waiting for transfers between devices, shards(): back = lax.all_to_all(back, 'lend', split_axis=0, concat_axis=0, tiled=True)  25.4 us
    all_to_all x1, waiting for transfers between devices, shards(): lax.all_to_all(asked, 'lend', split_axis=0, concat_axis=0, tiled=True)  19 us
    all_to_all x1, blocking collectives, shards(): lax.all_to_all(attended, 'tp', split_axis=0, concat_axis=0, tiled=True)  13.1 us
    all_to_all x1, starting transfers between devices, shards(): lax.all_to_all(asked, 'lend', split_axis=0, concat_axis=0, tiled=True)  10.6 us
    pallas_call x1, Pallas kernels, shards(): pl.pallas_call(lambda *refs: lent_kernel(*refs, rows=rows), out_shape=jax...  7.61 us
    all_to_all x1, starting transfers between devices, shards(): lax.all_to_all(packed, 'tp', split_axis=0, concat_axis=0, tiled=True)  6.71 us
    all_to_all x1, starting transfers between devices, shards(): back = lax.all_to_all(back, 'lend', split_axis=0, concat_axis=0, tiled=True)  6.51 us
    all_to_all x1, waiting for transfers between devices, shards(): lax.all_to_all(packed, 'tp', split_axis=0, concat_axis=0, tiled=True)  4.83 us
  transfers between devices with their start and end apart: 3, of which 3 were waited for; matrix products, arithmetic and copies ran while one was open for 4% of the time, Pallas kernels for 3%

profile of v3, /device:TPU:1, one launch (start us, length us, event | category | flops | bytes accessed | tf_op | source)
XLA Modules:
  0.0 109.2 jit_solution(6538197318933271195)
XLA Ops:
  0.0 1.7 %pack.1 = bf16[8,144,128]{2,1,0:T(8,128)(2,1)} custom-call(bf16[2,8,64,128]{3,2,1,0:T(8,128)(2,1)} %queries.1, bf16[64,128]{1,0:T(8,128)(2,1)} %bitcast.20, bf16[64,128]{1,0:T(8,128)(2,1)} %bitcast.21), custom_call_target="tpu_custom_call" | custom-call | tf_op jit(solution)/shard_map/pack/pallas_call | solution.py:345
  1.7 0.0 copy-start.4
  1.8 0.0 copy-start.5
  1.8 0.0 copy-start
  1.8 6.7 %all-to-all-start = ((bf16[8,144,128]{2,1,0:T(8,128)(2,1)}), bf16[8,144,128]{2,1,0:T(8,128)(2,1)S(1)}, u32[]{:S(2)}, u32[]{:S(2)}) async-start(bf16[8,144,128]{2,1,0:T(8,128)(2,1)} %pack.1), calls=%async_computation | async-start | bytes 589824 | tf_op jit(solution)/shard_map/all_to_all | solution.py:357
  8.5 0.7 broadcast_subtract_fusion
  9.2 0.1 sub.29
  9.3 0.1 fusion.5
  9.4 0.2 fusion.3
  9.6 0.7 fusion.6
  10.3 0.1 copy.16
  10.4 0.1 stack.14
  10.5 4.8 %all-to-all-done.refs_1_ = bf16[8,144,128]{2,1,0:T(8,128)(2,1)S(1)} async-done(((bf16[8,144,128]{2,1,0:T(8,128)(2,1)}), bf16[8,144,128]{2,1,0:T(8,128)(2,1)S(1)}, u32[]{:S(2)}, u32[]{:S(2)}) %all-to-all-start) | async-done | bytes 294944 | tf_op jit(solution)/shard_map/all_to_all | solution.py:357
  15.3 1.6 %pick.1.refs_5_ = bf16[32,128,128]{2,1,0:T(8,128)(2,1)} custom-call(s32[64]{0:T(128)S(1)} %get-tuple-element.11.refs_0_, bf16[1152,128]{1,0:T(8,128)(2,1)S(1)} %bitcast.14), custom_call_target="tpu_custom_call" | custom-call | tf_op jit(solution)/shard_map/pick/pallas_call | solution.py:396
  16.9 10.6 %all-to-all-start.1 = ((bf16[32,128,128]{2,1,0:T(8,128)(2,1)}), bf16[32,128,128]{2,1,0:T(8,128)(2,1)}, u32[]{:S(2)}, u32[]{:S(2)}) async-start(bf16[32,128,128]{2,1,0:T(8,128)(2,1)} %pick.1.refs_5_), calls=%async_computation.1 | async-start | bytes 2097152 | tf_op jit(solution)/shard_map/all_to_all | solution.py:408
  27.5 0.0 copy-done.4
  27.5 0.1 fusion.11
  27.6 0.2 convert_reduce_fusion.2
  27.8 0.0 copy-done.5
  27.8 0.2 select_reduce_fusion
  28.0 0.2 convert_reduce_fusion
  28.2 0.1 pad_add_fusion.2
  28.2 0.5 pad.9.refs_0_
  28.8 0.1 copy.17
  28.9 0.1 broadcast_in_dim.74
  29.0 0.1 reshape.88.refs_4_.refs_1_
  29.0 0.1 dynamic_slice.7.refs_0_
  29.1 0.0 copy-done
  29.1 0.0 copy-start.1
  29.1 1.6 %copy-done.1 = bf16[16,512,1,128]{3,1,2,0:T(8,128)(2,1)S(1)} copy-done((bf16[16,512,1,128]{3,1,2,0:T(8,128)(2,1)S(1)}, bf16[16,512,1,128]{3,1,2,0:T(8,128)(2,1)}, u32[]{:S(2)}) %copy-start.1) | copy-done | bytes 2097176
  30.7 2.9 %home.1 = (f32[16,64,128]{2,1,0:T(8,128)S(1)}, f32[16,128]{1,0:T(8,128)S(1)}) custom-call(s32[16]{0:T(128)S(1)} %dynamic_slice.7.refs_0_, bf16[8,144,128]{2,1,0:T(8,128)(2,1)S(1)} %all-to-all-done.refs_1_, bf16[16,512,128]{2,1,0:T(8,128)(2,1)S(1)} %bitcast.15, bf16[16,512,128]{2,1,0:T(8,128)(2,1)S(1)} %bitcast.16, s32[32,128]{1,0:T(8,128)S(1)} %reshape.88.refs_4_.refs_1_, ...), custom_call_target="tpu_custom_call" | custom-call | flops 268435456 | bytes 6291456 | tf_op jit(solution)/shard_map/home/pallas_call | solution.py:410
  33.7 0.0 copy-start.2
  33.7 0.6 copy-done.2
  34.3 19.0 %all-to-all-done.1.refs_1_ = bf16[32,128,128]{2,1,0:T(8,128)(2,1)} async-done(((bf16[32,128,128]{2,1,0:T(8,128)(2,1)}), bf16[32,128,128]{2,1,0:T(8,128)(2,1)}, u32[]{:S(2)}, u32[]{:S(2)}) %all-to-all-start.1) | async-done | bytes 1048608 | tf_op jit(solution)/shard_map/all_to_all | solution.py:408
  53.3 7.6 %lent.1 = bf16[32,136,128]{2,1,0:T(8,128)(2,1)} custom-call(s32[128]{0:T(128)} %pad.9.refs_0_, bf16[32,128,128]{2,1,0:T(8,128)(2,1)} %all-to-all-done.1.refs_1_, bf16[32,512,128]{2,1,0:T(8,128)(2,1)} %bitcast.17, bf16[32,512,128]{2,1,0:T(8,128)(2,1)} %bitcast.18, f32[16,128]{1,0:T(8,128)} %copy-done.2), custom_call_target="tpu_custom_call" | custom-call | tf_op jit(solution)/shard_map/lent/pallas_call | solution.py:436
  60.9 0.0 copy-start.3
  60.9 6.5 %all-to-all-start.2 = ((bf16[32,136,128]{2,1,0:T(8,128)(2,1)}), bf16[32,136,128]{2,1,0:T(8,128)(2,1)S(1)}, u32[]{:S(2)}, u32[]{:S(2)}) async-start(bf16[32,136,128]{2,1,0:T(8,128)(2,1)} %lent.1), calls=%async_computation.2 | async-start | bytes 2228224 | tf_op jit(solution)/shard_map/all_to_all | solution.py:459
  67.4 0.1 convert_reduce_fusion.1
  67.5 0.1 select_reduce_fusion.2
  67.7 0.7 pad_add_fusion.1
  68.4 25.4 %all-to-all-done.2.refs_2_ = bf16[32,136,128]{2,1,0:T(8,128)(2,1)S(1)} async-done(((bf16[32,136,128]{2,1,0:T(8,128)(2,1)}), bf16[32,136,128]{2,1,0:T(8,128)(2,1)S(1)}, u32[]{:S(2)}, u32[]{:S(2)}) %all-to-all-start.2) | async-done | bytes 1114144 | tf_op jit(solution)/shard_map/all_to_all | solution.py:459
  93.8 0.0 copy-done.3
  93.8 1.6 %combine.1 = bf16[8,128,128]{2,1,0:T(8,128)(2,1)S(1)} custom-call(s32[256]{0:T(256)S(1)} %pad.8.refs_0_, s32[32,128]{1,0:T(8,128)S(1)} %reshape.88.refs_4_.refs_1_, bf16[32,136,128]{2,1,0:T(8,128)(2,1)S(1)} %all-to-all-done.2.refs_2_, f32[16,64,128]{2,1,0:T(8,128)S(1)} %get-tuple-element.8.refs_3_, f32[16,128]{1,0:T(8,128)S(1)} %copy-done.3), custom_call_target="tpu_custom_call" | custom-call | tf_op jit(solution)/shard_map/combine/pallas_call | solution.py:461
  95.4 13.1 %all_to_all.20 = bf16[8,128,128]{2,1,0:T(8,128)(2,1)S(1)} all-to-all(bf16[8,128,128]{2,1,0:T(8,128)(2,1)S(1)} %combine.1), channel_id=1, replica_groups=mesh['lend'=32,'tp'=8] {'tp'}, dimensions={0} | all-to-all | bytes 524288 | tf_op jit(solution)/shard_map/all_to_all | solution.py:475
  108.5 0.7 copy.20
  (5 shorter events, 0.0 us)
Async XLA Ops:
  1.7 25.7 %copy-start.4 = (s32[1024]{0:T(1024)S(1)}, s32[1024]{0:T(1024)}, u32[]{:S(2)}) copy-start(s32[1024]{0:T(1024)} %param.17) | copy-start | bytes 12292
  1.8 26.0 %copy-start.5 = (s32[512]{0:T(512)S(1)}, s32[512]{0:T(512)}, u32[]{:S(2)}) copy-start(s32[512]{0:T(512)} %param.16) | copy-start | bytes 6148
  1.8 27.4 %copy-start = (bf16[16,512,1,128]{3,1,2,0:T(8,128)(2,1)S(1)}, bf16[16,512,1,128]{3,1,2,0:T(8,128)(2,1)}, u32[]{:S(2)}) copy-start(bf16[16,512,1,128]{3,1,2,0:T(8,128)(2,1)} %param.12) | copy-start | bytes 6291460
  1.8 13.5 %all-to-all-start = ((bf16[8,144,128]{2,1,0:T(8,128)(2,1)}), bf16[8,144,128]{2,1,0:T(8,128)(2,1)S(1)}, u32[]{:S(2)}, u32[]{:S(2)}) async-start(bf16[8,144,128]{2,1,0:T(8,128)(2,1)} %pack.1), calls=%async_computation | async-start | bytes 589824 | tf_op jit(solution)/shard_map/all_to_all | solution.py:357
  16.9 36.3 %all-to-all-start.1 = ((bf16[32,128,128]{2,1,0:T(8,128)(2,1)}), bf16[32,128,128]{2,1,0:T(8,128)(2,1)}, u32[]{:S(2)}, u32[]{:S(2)}) async-start(bf16[32,128,128]{2,1,0:T(8,128)(2,1)} %pick.1.refs_5_), calls=%async_computation.1 | async-start | bytes 2097152 | tf_op jit(solution)/shard_map/all_to_all | solution.py:408
  29.1 1.6 %copy-start.1 = (bf16[16,512,1,128]{3,1,2,0:T(8,128)(2,1)S(1)}, bf16[16,512,1,128]{3,1,2,0:T(8,128)(2,1)}, u32[]{:S(2)}) copy-start(bf16[16,512,1,128]{3,1,2,0:T(8,128)(2,1)} %param.13) | copy-start | bytes 6291460
  33.7 0.6 copy-start.2
  60.9 32.9 %copy-start.3 = (f32[16,128]{1,0:T(8,128)S(1)}, f32[16,128]{1,0:T(8,128)}, u32[]{:S(2)}) copy-start(f32[16,128]{1,0:T(8,128)} %copy-done.2) | copy-start | bytes 24580
  60.9 32.9 %all-to-all-start.2 = ((bf16[32,136,128]{2,1,0:T(8,128)(2,1)}), bf16[32,136,128]{2,1,0:T(8,128)(2,1)S(1)}, u32[]{:S(2)}, u32[]{:S(2)}) async-start(bf16[32,136,128]{2,1,0:T(8,128)(2,1)} %lent.1), calls=%async_computation.2 | async-start | bytes 2228224 | tf_op jit(solution)/shard_map/all_to_all | solution.py:459

commit v4 on v3

--- a/solution.py
+++ b/solution.py
@@ -151,19 +151,17 @@
 
 
 def lent_kernel(
-    info_hbm,
+    info,
     query_hbm,
     keys_hbm,
     values_hbm,
     home_lse,
     out_ref,
-    info,
     queries,
     keys,
     values,
     stats,
     sems,
-    ends,
     *,
     rows,
 ):
@@ -178,19 +176,15 @@
         part = pl.ds(chunk * group, group)
         return pltpu.make_async_copy(source.at[part], target.at[part], sems.at[chunk, kind])
 
-    arrivals = [
-        pltpu.make_async_copy(info_hbm, info, ends.at[0]),
-        pltpu.make_async_copy(query_hbm, queries, ends.at[1]),
-    ]
-    for arrival in arrivals:
-        arrival.start()
+    arrival = pltpu.make_async_copy(query_hbm, queries, sems.at[chunks, 0])
+    arrival.start()
     for chunk in range(chunks):
         for kind in range(2):
             copy(kind, chunk).start()
     stats[...] = jnp.zeros_like(stats)
     lane = lax.broadcasted_iota(jnp.int32, (rows, stats.shape[1]), 1)
-    for arrival in arrivals:
-        arrival.wait()
+    position = lax.broadcasted_iota(jnp.int32, (1, BLOCK), 1)
+    arrival.wait()
 
     def some(chunk, carry):
         for kind in range(2):
@@ -201,24 +195,23 @@
             place = info[slot]
             length = info[slots + slot]
             home = lax.div(place, CAP)
-            start = pl.multiple_of(lax.rem(place, CAP) * rows, rows)
-            raw = nt_dot(queries[home, pl.ds(start, rows), :], keys[slot])
-            position = lax.broadcasted_iota(jnp.int32, raw.shape, 1)
-            scores.append(jnp.where(position < length, raw, NEG_BIG))
-            placed.append((home, start))
+            first = pl.multiple_of(lax.rem(place, CAP) * rows, rows)
+            raw = nt_dot(queries[home, pl.ds(first, rows), :], keys[slot])
+            scores.append(raw + jnp.where(position < length, 0.0, NEG_BIG))
+            placed.append((home, first))
         tops = [jnp.max(old, axis=1, keepdims=True) for old in scores]
         for near in range(group):
             terms = jnp.exp2((scores[near] - tops[near]) * (factor * LOG2E))
             total.append(jnp.sum(terms, axis=1, keepdims=True))
             mixed.append(nn_dot(terms.astype(jnp.bfloat16), values[chunk * group + near]))
-        for near, (home, start) in enumerate(placed):
-            out_ref[home, pl.ds(start, rows), :] = (mixed[near] * (1.0 / total[near])).astype(
+        for near, (home, first) in enumerate(placed):
+            out_ref[home, pl.ds(first, rows), :] = (mixed[near] * (1.0 / total[near])).astype(
                 jnp.bfloat16
             )
-            stats[pl.ds(start, rows), :] = jnp.where(
+            stats[pl.ds(first, rows), :] = jnp.where(
                 lane == home,
                 tops[near] * factor + jnp.log(total[near]),
-                stats[pl.ds(start, rows), :],
+                stats[pl.ds(first, rows), :],
             )
         return carry
 
@@ -385,7 +378,7 @@
     before = slot[None, :] < slot[:, None]
     rank = jnp.sum((home[None, :] == home[:, None]) & before, axis=1, dtype=jnp.int32)
     place = jnp.where(own >= 0, home * CAP + rank, me * CAP)
-    lent_info = padded(jnp.concatenate([place, jnp.where(own >= 0, length, 0)]))
+    lent_info = jnp.concatenate([place, jnp.where(own >= 0, length, 0)])
     place_info = padded(
         listed(picks >= 0, [jnp.arange(lend_count * CAP, dtype=jnp.int32), picks])
     )
@@ -436,16 +429,14 @@
     back = pl.pallas_call(
         lambda *refs: lent_kernel(*refs, rows=rows),
         out_shape=jax.ShapeDtypeStruct(back_shape, jnp.bfloat16),
-        in_specs=[spec(HBM)] * 5,
+        in_specs=[spec(SMEM)] + [spec(HBM)] * 4,
         out_specs=spec(VMEM),
         scratch_shapes=[
-            pltpu.SMEM(lent_info.shape, jnp.int32),
             pltpu.VMEM((lend_count, CAP * rows, dim), jnp.bfloat16),
             pltpu.VMEM((slots, BLOCK, dim), jnp.bfloat16),
             pltpu.VMEM((slots, BLOCK, dim), jnp.bfloat16),
             pltpu.VMEM((CAP * rows, LANES), jnp.float32),
-            pltpu.SemaphoreType.DMA((max(slots // LENT_GROUP, 1), 2)),
-            pltpu.SemaphoreType.DMA((2,)),
+            pltpu.SemaphoreType.DMA((max(slots // LENT_GROUP, 1) + 1, 2)),
         ],
         compiler_params=params(LENT_MIB),
         name="lent",

time: 110 us -> 109 us (level)
  no operation moved by 1% of the time
where the time goes in v4:
time: 109 us; the launch traced here: 108 us
  waiting for transfers between devices  49.2 us (45%)
  starting transfers between devices  23.8 us (22%)
  Pallas kernels  14.6 us (13%)
  blocking collectives  13.1 us (12%)
  other arithmetic  3.91 us (4%)
  local copies, waits for them, and re-layouts  3.55 us (3%)
    all_to_all x1, waiting for transfers between devices, shards(): back = lax.all_to_all(back, 'lend', split_axis=0, concat_axis=0, tiled=True)  25.4 us
    all_to_all x1, waiting for transfers between devices, shards(): lax.all_to_all(asked, 'lend', split_axis=0, concat_axis=0, tiled=True)  19 us
    all_to_all x1, blocking collectives, shards(): lax.all_to_all(attended, 'tp', split_axis=0, concat_axis=0, tiled=True)  13.1 us
    all_to_all x1, starting transfers between devices, shards(): lax.all_to_all(asked, 'lend', split_axis=0, concat_axis=0, tiled=True)  10.6 us
    pallas_call x1, Pallas kernels, shards(): pl.pallas_call(lambda *refs: lent_kernel(*refs, rows=rows), out_shape=jax...  6.72 us
    all_to_all x1, starting transfers between devices, shards(): lax.all_to_all(packed, 'tp', split_axis=0, concat_axis=0, tiled=True)  6.71 us
    all_to_all x1, starting transfers between devices, shards(): back = lax.all_to_all(back, 'lend', split_axis=0, concat_axis=0, tiled=True)  6.52 us
    all_to_all x1, waiting for transfers between devices, shards(): lax.all_to_all(packed, 'tp', split_axis=0, concat_axis=0, tiled=True)  4.83 us
  transfers between devices with their start and end apart: 3, of which 3 were waited for; matrix products, arithmetic and copies ran while one was open for 4% of the time, Pallas kernels for 3%

profile of v4, /device:TPU:1, one launch (start us, length us, event | category | flops | bytes accessed | tf_op | source)
XLA Modules:
  0.0 108.3 jit_solution(17103957811447683791)
XLA Ops:
  0.0 1.7 %pack.1 = bf16[8,144,128]{2,1,0:T(8,128)(2,1)} custom-call(bf16[2,8,64,128]{3,2,1,0:T(8,128)(2,1)} %queries.1, bf16[64,128]{1,0:T(8,128)(2,1)} %bitcast.20, bf16[64,128]{1,0:T(8,128)(2,1)} %bitcast.21), custom_call_target="tpu_custom_call" | custom-call | tf_op jit(solution)/shard_map/pack/pallas_call | solution.py:338
  1.7 0.0 copy-start.5
  1.8 0.0 copy-start.4
  1.8 0.0 copy-start
  1.8 6.7 %all-to-all-start = ((bf16[8,144,128]{2,1,0:T(8,128)(2,1)}), bf16[8,144,128]{2,1,0:T(8,128)(2,1)S(1)}, u32[]{:S(2)}, u32[]{:S(2)}) async-start(bf16[8,144,128]{2,1,0:T(8,128)(2,1)} %pack.1), calls=%async_computation | async-start | bytes 589824 | tf_op jit(solution)/shard_map/all_to_all | solution.py:350
  8.5 0.7 broadcast_subtract_fusion
  9.2 0.1 sub.29
  9.3 0.1 fusion.5
  9.4 0.2 fusion.3
  9.6 0.7 fusion.6
  10.3 0.1 copy.16
  10.4 0.1 stack.14
  10.5 4.8 %all-to-all-done.refs_1_ = bf16[8,144,128]{2,1,0:T(8,128)(2,1)S(1)} async-done(((bf16[8,144,128]{2,1,0:T(8,128)(2,1)}), bf16[8,144,128]{2,1,0:T(8,128)(2,1)S(1)}, u32[]{:S(2)}, u32[]{:S(2)}) %all-to-all-start) | async-done | bytes 294944 | tf_op jit(solution)/shard_map/all_to_all | solution.py:350
  15.3 1.6 %pick.1.refs_5_ = bf16[32,128,128]{2,1,0:T(8,128)(2,1)} custom-call(s32[64]{0:T(128)S(1)} %get-tuple-element.11.refs_0_, bf16[1152,128]{1,0:T(8,128)(2,1)S(1)} %bitcast.14), custom_call_target="tpu_custom_call" | custom-call | tf_op jit(solution)/shard_map/pick/pallas_call | solution.py:389
  16.9 10.6 %all-to-all-start.1 = ((bf16[32,128,128]{2,1,0:T(8,128)(2,1)}), bf16[32,128,128]{2,1,0:T(8,128)(2,1)}, u32[]{:S(2)}, u32[]{:S(2)}) async-start(bf16[32,128,128]{2,1,0:T(8,128)(2,1)} %pick.1.refs_5_), calls=%async_computation.1 | async-start | bytes 2097152 | tf_op jit(solution)/shard_map/all_to_all | solution.py:401
  27.5 0.1 copy.17
  27.6 0.1 broadcast_in_dim.74
  27.7 0.1 reshape.88.refs_4_.refs_1_
  27.8 0.0 copy-done.5
  27.8 0.1 dynamic_slice.7.refs_0_
  27.8 0.0 copy-done.4
  27.8 0.1 fusion.11
  27.9 0.2 convert_reduce_fusion.2
  28.1 0.2 select_reduce_fusion
  28.3 0.2 convert_reduce_fusion
  28.5 0.6 pad_add_fusion.2.refs_0_
  29.1 0.0 copy-done
  29.1 0.0 copy-start.1
  29.1 1.6 %copy-done.1 = bf16[16,512,1,128]{3,1,2,0:T(8,128)(2,1)S(1)} copy-done((bf16[16,512,1,128]{3,1,2,0:T(8,128)(2,1)S(1)}, bf16[16,512,1,128]{3,1,2,0:T(8,128)(2,1)}, u32[]{:S(2)}) %copy-start.1) | copy-done | bytes 2097176
  30.7 2.9 %home.1 = (f32[16,64,128]{2,1,0:T(8,128)S(1)}, f32[16,128]{1,0:T(8,128)S(1)}) custom-call(s32[16]{0:T(128)S(1)} %dynamic_slice.7.refs_0_, bf16[8,144,128]{2,1,0:T(8,128)(2,1)S(1)} %all-to-all-done.refs_1_, bf16[16,512,128]{2,1,0:T(8,128)(2,1)S(1)} %bitcast.15, bf16[16,512,128]{2,1,0:T(8,128)(2,1)S(1)} %bitcast.16, s32[32,128]{1,0:T(8,128)S(1)} %reshape.88.refs_4_.refs_1_, ...), custom_call_target="tpu_custom_call" | custom-call | flops 268435456 | bytes 6291456 | tf_op jit(solution)/shard_map/home/pallas_call | solution.py:403
  33.6 0.0 copy-start.2
  33.6 0.6 copy-done.2
  34.2 19.0 %all-to-all-done.1.refs_1_ = bf16[32,128,128]{2,1,0:T(8,128)(2,1)} async-done(((bf16[32,128,128]{2,1,0:T(8,128)(2,1)}), bf16[32,128,128]{2,1,0:T(8,128)(2,1)}, u32[]{:S(2)}, u32[]{:S(2)}) %all-to-all-start.1) | async-done | bytes 1048608 | tf_op jit(solution)/shard_map/all_to_all | solution.py:401
  53.3 6.7 %lent.1 = bf16[32,136,128]{2,1,0:T(8,128)(2,1)} custom-call(s32[64]{0:T(128)} %pad_add_fusion.2.refs_0_, bf16[32,128,128]{2,1,0:T(8,128)(2,1)} %all-to-all-done.1.refs_1_, bf16[32,512,128]{2,1,0:T(8,128)(2,1)} %bitcast.17, bf16[32,512,128]{2,1,0:T(8,128)(2,1)} %bitcast.18, f32[16,128]{1,0:T(8,128)} %copy-done.2), custom_call_target="tpu_custom_call" | custom-call | tf_op jit(solution)/shard_map/lent/pallas_call | solution.py:429
  60.0 0.0 copy-start.3
  60.0 6.5 %all-to-all-start.2 = ((bf16[32,136,128]{2,1,0:T(8,128)(2,1)}), bf16[32,136,128]{2,1,0:T(8,128)(2,1)S(1)}, u32[]{:S(2)}, u32[]{:S(2)}) async-start(bf16[32,136,128]{2,1,0:T(8,128)(2,1)} %lent.1), calls=%async_computation.2 | async-start | bytes 2228224 | tf_op jit(solution)/shard_map/all_to_all | solution.py:450
  66.5 0.1 convert_reduce_fusion.1
  66.7 0.1 select_reduce_fusion.2
  66.8 0.7 pad_add_fusion.1
  67.5 25.4 %all-to-all-done.2.refs_2_ = bf16[32,136,128]{2,1,0:T(8,128)(2,1)S(1)} async-done(((bf16[32,136,128]{2,1,0:T(8,128)(2,1)}), bf16[32,136,128]{2,1,0:T(8,128)(2,1)S(1)}, u32[]{:S(2)}, u32[]{:S(2)}) %all-to-all-start.2) | async-done | bytes 1114144 | tf_op jit(solution)/shard_map/all_to_all | solution.py:450
  92.8 0.0 copy-done.3
  92.8 1.6 %combine.1 = bf16[8,128,128]{2,1,0:T(8,128)(2,1)S(1)} custom-call(s32[256]{0:T(256)S(1)} %pad.4.refs_0_, s32[32,128]{1,0:T(8,128)S(1)} %reshape.88.refs_4_.refs_1_, bf16[32,136,128]{2,1,0:T(8,128)(2,1)S(1)} %all-to-all-done.2.refs_2_, f32[16,64,128]{2,1,0:T(8,128)S(1)} %get-tuple-element.8.refs_3_, f32[16,128]{1,0:T(8,128)S(1)} %copy-done.3), custom_call_target="tpu_custom_call" | custom-call | tf_op jit(solution)/shard_map/combine/pallas_call | solution.py:452
  94.4 13.1 %all_to_all.20 = bf16[8,128,128]{2,1,0:T(8,128)(2,1)S(1)} all-to-all(bf16[8,128,128]{2,1,0:T(8,128)(2,1)S(1)} %combine.1), channel_id=1, replica_groups=mesh['lend'=32,'tp'=8] {'tp'}, dimensions={0} | all-to-all | bytes 524288 | tf_op jit(solution)/shard_map/all_to_all | solution.py:466
  107.6 0.7 copy.20
  (5 shorter events, 0.0 us)
Async XLA Ops:
  1.7 26.0 %copy-start.5 = (s32[512]{0:T(512)S(1)}, s32[512]{0:T(512)}, u32[]{:S(2)}) copy-start(s32[512]{0:T(512)} %param.16) | copy-start | bytes 6148
  1.8 26.1 %copy-start.4 = (s32[1024]{0:T(1024)S(1)}, s32[1024]{0:T(1024)}, u32[]{:S(2)}) copy-start(s32[1024]{0:T(1024)} %param.17) | copy-start | bytes 12292
  1.8 27.3 %copy-start = (bf16[16,512,1,128]{3,1,2,0:T(8,128)(2,1)S(1)}, bf16[16,512,1,128]{3,1,2,0:T(8,128)(2,1)}, u32[]{:S(2)}) copy-start(bf16[16,512,1,128]{3,1,2,0:T(8,128)(2,1)} %param.12) | copy-start | bytes 6291460
  1.8 13.5 %all-to-all-start = ((bf16[8,144,128]{2,1,0:T(8,128)(2,1)}), bf16[8,144,128]{2,1,0:T(8,128)(2,1)S(1)}, u32[]{:S(2)}, u32[]{:S(2)}) async-start(bf16[8,144,128]{2,1,0:T(8,128)(2,1)} %pack.1), calls=%async_computation | async-start | bytes 589824 | tf_op jit(solution)/shard_map/all_to_all | solution.py:350
  16.9 36.3 %all-to-all-start.1 = ((bf16[32,128,128]{2,1,0:T(8,128)(2,1)}), bf16[32,128,128]{2,1,0:T(8,128)(2,1)}, u32[]{:S(2)}, u32[]{:S(2)}) async-start(bf16[32,128,128]{2,1,0:T(8,128)(2,1)} %pick.1.refs_5_), calls=%async_computation.1 | async-start | bytes 2097152 | tf_op jit(solution)/shard_map/all_to_all | solution.py:401
  29.1 1.6 %copy-start.1 = (bf16[16,512,1,128]{3,1,2,0:T(8,128)(2,1)S(1)}, bf16[16,512,1,128]{3,1,2,0:T(8,128)(2,1)}, u32[]{:S(2)}) copy-start(bf16[16,512,1,128]{3,1,2,0:T(8,128)(2,1)} %param.13) | copy-start | bytes 6291460
  33.6 0.6 copy-start.2
  60.0 32.9 %copy-start.3 = (f32[16,128]{1,0:T(8,128)S(1)}, f32[16,128]{1,0:T(8,128)}, u32[]{:S(2)}) copy-start(f32[16,128]{1,0:T(8,128)} %copy-done.2) | copy-start | bytes 24580
  60.0 32.8 %all-to-all-start.2 = ((bf16[32,136,128]{2,1,0:T(8,128)(2,1)}), bf16[32,136,128]{2,1,0:T(8,128)(2,1)S(1)}, u32[]{:S(2)}, u32[]{:S(2)}) async-start(bf16[32,136,128]{2,1,0:T(8,128)(2,1)} %lent.1), calls=%async_computation.2 | async-start | bytes 2228224 | tf_op jit(solution)/shard_map/all_to_all | solution.py:450

commit v5 on v4

--- a/solution.py
+++ b/solution.py
@@ -13,7 +13,7 @@
 BLOCK = 512
 STAT_ROWS = 8
 LANES = 128
-LENT_GROUP = 8
+LENT_GROUP = 16
 HOME_GROUP = 2
 MERGE_GROUP = 4
 LENT_MIB = 58

time: 109 us -> 109 us (level)
  no operation moved by 1% of the time
where the time goes in v5:
time: 109 us; the launch traced here: 108 us
  waiting for transfers between devices  49.1 us (45%)
  starting transfers between devices  23.8 us (22%)
  Pallas kernels  14.7 us (13%)
  blocking collectives  13.2 us (12%)
  other arithmetic  3.91 us (4%)
  local copies, waits for them, and re-layouts  3.55 us (3%)
    all_to_all x1, waiting for transfers between devices, shards(): back = lax.all_to_all(back, 'lend', split_axis=0, concat_axis=0, tiled=True)  25.3 us
    all_to_all x1, waiting for transfers between devices, shards(): lax.all_to_all(asked, 'lend', split_axis=0, concat_axis=0, tiled=True)  19 us
    all_to_all x1, blocking collectives, shards(): lax.all_to_all(attended, 'tp', split_axis=0, concat_axis=0, tiled=True)  13.2 us
    all_to_all x1, starting transfers between devices, shards(): lax.all_to_all(asked, 'lend', split_axis=0, concat_axis=0, tiled=True)  10.6 us
    pallas_call x1, Pallas kernels, shards(): pl.pallas_call(lambda *refs: lent_kernel(*refs, rows=rows), out_shape=jax...  6.86 us
    all_to_all x1, starting transfers between devices, shards(): lax.all_to_all(packed, 'tp', split_axis=0, concat_axis=0, tiled=True)  6.71 us
    all_to_all x1, starting transfers between devices, shards(): back = lax.all_to_all(back, 'lend', split_axis=0, concat_axis=0, tiled=True)  6.52 us
    all_to_all x1, waiting for transfers between devices, shards(): lax.all_to_all(packed, 'tp', split_axis=0, concat_axis=0, tiled=True)  4.83 us
  transfers between devices with their start and end apart: 3, of which 3 were waited for; matrix products, arithmetic and copies ran while one was open for 4% of the time, Pallas kernels for 3%

profile of v5, /device:TPU:1, one launch (start us, length us, event | category | flops | bytes accessed | tf_op | source)
XLA Modules:
  0.0 108.4 jit_solution(6651394775594219262)
XLA Ops:
  0.0 1.7 %pack.1 = bf16[8,144,128]{2,1,0:T(8,128)(2,1)} custom-call(bf16[2,8,64,128]{3,2,1,0:T(8,128)(2,1)} %queries.1, bf16[64,128]{1,0:T(8,128)(2,1)} %bitcast.20, bf16[64,128]{1,0:T(8,128)(2,1)} %bitcast.21), custom_call_target="tpu_custom_call" | custom-call | tf_op jit(solution)/shard_map/pack/pallas_call | solution.py:338
  1.7 0.0 copy-start.5
  1.8 0.0 copy-start.4
  1.8 0.0 copy-start
  1.8 6.7 %all-to-all-start = ((bf16[8,144,128]{2,1,0:T(8,128)(2,1)}), bf16[8,144,128]{2,1,0:T(8,128)(2,1)S(1)}, u32[]{:S(2)}, u32[]{:S(2)}) async-start(bf16[8,144,128]{2,1,0:T(8,128)(2,1)} %pack.1), calls=%async_computation | async-start | bytes 589824 | tf_op jit(solution)/shard_map/all_to_all | solution.py:350
  8.5 0.7 broadcast_subtract_fusion
  9.2 0.1 sub.29
  9.3 0.1 fusion.5
  9.4 0.2 fusion.3
  9.6 0.7 fusion.6
  10.3 0.1 copy.16
  10.4 0.1 stack.14
  10.5 4.8 %all-to-all-done.refs_1_ = bf16[8,144,128]{2,1,0:T(8,128)(2,1)S(1)} async-done(((bf16[8,144,128]{2,1,0:T(8,128)(2,1)}), bf16[8,144,128]{2,1,0:T(8,128)(2,1)S(1)}, u32[]{:S(2)}, u32[]{:S(2)}) %all-to-all-start) | async-done | bytes 294944 | tf_op jit(solution)/shard_map/all_to_all | solution.py:350
  15.3 1.6 %pick.1.refs_5_ = bf16[32,128,128]{2,1,0:T(8,128)(2,1)} custom-call(s32[64]{0:T(128)S(1)} %get-tuple-element.11.refs_0_, bf16[1152,128]{1,0:T(8,128)(2,1)S(1)} %bitcast.14), custom_call_target="tpu_custom_call" | custom-call | tf_op jit(solution)/shard_map/pick/pallas_call | solution.py:389
  16.9 10.6 %all-to-all-start.1 = ((bf16[32,128,128]{2,1,0:T(8,128)(2,1)}), bf16[32,128,128]{2,1,0:T(8,128)(2,1)}, u32[]{:S(2)}, u32[]{:S(2)}) async-start(bf16[32,128,128]{2,1,0:T(8,128)(2,1)} %pick.1.refs_5_), calls=%async_computation.1 | async-start | bytes 2097152 | tf_op jit(solution)/shard_map/all_to_all | solution.py:401
  27.5 0.1 copy.17
  27.6 0.1 broadcast_in_dim.74
  27.7 0.1 reshape.88.refs_4_.refs_1_
  27.8 0.0 copy-done.5
  27.8 0.1 dynamic_slice.7.refs_0_
  27.8 0.0 copy-done.4
  27.8 0.1 fusion.11
  27.9 0.2 convert_reduce_fusion.2
  28.1 0.2 select_reduce_fusion
  28.3 0.2 convert_reduce_fusion
  28.5 0.6 pad_add_fusion.2.refs_0_
  29.1 0.0 copy-done
  29.1 0.0 copy-start.1
  29.1 1.6 %copy-done.1 = bf16[16,512,1,128]{3,1,2,0:T(8,128)(2,1)S(1)} copy-done((bf16[16,512,1,128]{3,1,2,0:T(8,128)(2,1)S(1)}, bf16[16,512,1,128]{3,1,2,0:T(8,128)(2,1)}, u32[]{:S(2)}) %copy-start.1) | copy-done | bytes 2097176
  30.7 2.9 %home.1 = (f32[16,64,128]{2,1,0:T(8,128)S(1)}, f32[16,128]{1,0:T(8,128)S(1)}) custom-call(s32[16]{0:T(128)S(1)} %dynamic_slice.7.refs_0_, bf16[8,144,128]{2,1,0:T(8,128)(2,1)S(1)} %all-to-all-done.refs_1_, bf16[16,512,128]{2,1,0:T(8,128)(2,1)S(1)} %bitcast.15, bf16[16,512,128]{2,1,0:T(8,128)(2,1)S(1)} %bitcast.16, s32[32,128]{1,0:T(8,128)S(1)} %reshape.88.refs_4_.refs_1_, ...), custom_call_target="tpu_custom_call" | custom-call | flops 268435456 | bytes 6291456 | tf_op jit(solution)/shard_map/home/pallas_call | solution.py:403
  33.6 0.0 copy-start.2
  33.6 0.6 copy-done.2
  34.2 19.0 %all-to-all-done.1.refs_1_ = bf16[32,128,128]{2,1,0:T(8,128)(2,1)} async-done(((bf16[32,128,128]{2,1,0:T(8,128)(2,1)}), bf16[32,128,128]{2,1,0:T(8,128)(2,1)}, u32[]{:S(2)}, u32[]{:S(2)}) %all-to-all-start.1) | async-done | bytes 1048608 | tf_op jit(solution)/shard_map/all_to_all | solution.py:401
  53.3 6.9 %lent.1 = bf16[32,136,128]{2,1,0:T(8,128)(2,1)} custom-call(s32[64]{0:T(128)} %pad_add_fusion.2.refs_0_, bf16[32,128,128]{2,1,0:T(8,128)(2,1)} %all-to-all-done.1.refs_1_, bf16[32,512,128]{2,1,0:T(8,128)(2,1)} %bitcast.17, bf16[32,512,128]{2,1,0:T(8,128)(2,1)} %bitcast.18, f32[16,128]{1,0:T(8,128)} %copy-done.2), custom_call_target="tpu_custom_call" | custom-call | tf_op jit(solution)/shard_map/lent/pallas_call | solution.py:429
  60.1 0.0 copy-start.3
  60.1 6.5 %all-to-all-start.2 = ((bf16[32,136,128]{2,1,0:T(8,128)(2,1)}), bf16[32,136,128]{2,1,0:T(8,128)(2,1)S(1)}, u32[]{:S(2)}, u32[]{:S(2)}) async-start(bf16[32,136,128]{2,1,0:T(8,128)(2,1)} %lent.1), calls=%async_computation.2 | async-start | bytes 2228224 | tf_op jit(solution)/shard_map/all_to_all | solution.py:450
  66.7 0.1 convert_reduce_fusion.1
  66.8 0.1 select_reduce_fusion.2
  66.9 0.7 pad_add_fusion.1
  67.6 25.3 %all-to-all-done.2.refs_2_ = bf16[32,136,128]{2,1,0:T(8,128)(2,1)S(1)} async-done(((bf16[32,136,128]{2,1,0:T(8,128)(2,1)}), bf16[32,136,128]{2,1,0:T(8,128)(2,1)S(1)}, u32[]{:S(2)}, u32[]{:S(2)}) %all-to-all-start.2) | async-done | bytes 1114144 | tf_op jit(solution)/shard_map/all_to_all | solution.py:450
  92.9 0.0 copy-done.3
  92.9 1.5 %combine.1 = bf16[8,128,128]{2,1,0:T(8,128)(2,1)S(1)} custom-call(s32[256]{0:T(256)S(1)} %pad.4.refs_0_, s32[32,128]{1,0:T(8,128)S(1)} %reshape.88.refs_4_.refs_1_, bf16[32,136,128]{2,1,0:T(8,128)(2,1)S(1)} %all-to-all-done.2.refs_2_, f32[16,64,128]{2,1,0:T(8,128)S(1)} %get-tuple-element.8.refs_3_, f32[16,128]{1,0:T(8,128)S(1)} %copy-done.3), custom_call_target="tpu_custom_call" | custom-call | tf_op jit(solution)/shard_map/combine/pallas_call | solution.py:452
  94.5 13.2 %all_to_all.20 = bf16[8,128,128]{2,1,0:T(8,128)(2,1)S(1)} all-to-all(bf16[8,128,128]{2,1,0:T(8,128)(2,1)S(1)} %combine.1), channel_id=1, replica_groups=mesh['lend'=32,'tp'=8] {'tp'}, dimensions={0} | all-to-all | bytes 524288 | tf_op jit(solution)/shard_map/all_to_all | solution.py:466
  107.7 0.7 copy.20
  (5 shorter events, 0.0 us)
Async XLA Ops:
  1.7 26.0 %copy-start.5 = (s32[512]{0:T(512)S(1)}, s32[512]{0:T(512)}, u32[]{:S(2)}) copy-start(s32[512]{0:T(512)} %param.16) | copy-start | bytes 6148
  1.8 26.1 %copy-start.4 = (s32[1024]{0:T(1024)S(1)}, s32[1024]{0:T(1024)}, u32[]{:S(2)}) copy-start(s32[1024]{0:T(1024)} %param.17) | copy-start | bytes 12292
  1.8 27.3 %copy-start = (bf16[16,512,1,128]{3,1,2,0:T(8,128)(2,1)S(1)}, bf16[16,512,1,128]{3,1,2,0:T(8,128)(2,1)}, u32[]{:S(2)}) copy-start(bf16[16,512,1,128]{3,1,2,0:T(8,128)(2,1)} %param.12) | copy-start | bytes 6291460
  1.8 13.5 %all-to-all-start = ((bf16[8,144,128]{2,1,0:T(8,128)(2,1)}), bf16[8,144,128]{2,1,0:T(8,128)(2,1)S(1)}, u32[]{:S(2)}, u32[]{:S(2)}) async-start(bf16[8,144,128]{2,1,0:T(8,128)(2,1)} %pack.1), calls=%async_computation | async-start | bytes 589824 | tf_op jit(solution)/shard_map/all_to_all | solution.py:350
  16.9 36.3 %all-to-all-start.1 = ((bf16[32,128,128]{2,1,0:T(8,128)(2,1)}), bf16[32,128,128]{2,1,0:T(8,128)(2,1)}, u32[]{:S(2)}, u32[]{:S(2)}) async-start(bf16[32,128,128]{2,1,0:T(8,128)(2,1)} %pick.1.refs_5_), calls=%async_computation.1 | async-start | bytes 2097152 | tf_op jit(solution)/shard_map/all_to_all | solution.py:401
  29.1 1.6 %copy-start.1 = (bf16[16,512,1,128]{3,1,2,0:T(8,128)(2,1)S(1)}, bf16[16,512,1,128]{3,1,2,0:T(8,128)(2,1)}, u32[]{:S(2)}) copy-start(bf16[16,512,1,128]{3,1,2,0:T(8,128)(2,1)} %param.13) | copy-start | bytes 6291460
  33.6 0.6 copy-start.2
  60.1 32.8 %copy-start.3 = (f32[16,128]{1,0:T(8,128)S(1)}, f32[16,128]{1,0:T(8,128)}, u32[]{:S(2)}) copy-start(f32[16,128]{1,0:T(8,128)} %copy-done.2) | copy-start | bytes 24580
  60.1 32.8 %all-to-all-start.2 = ((bf16[32,136,128]{2,1,0:T(8,128)(2,1)}), bf16[32,136,128]{2,1,0:T(8,128)(2,1)S(1)}, u32[]{:S(2)}, u32[]{:S(2)}) async-start(bf16[32,136,128]{2,1,0:T(8,128)(2,1)} %lent.1), calls=%async_computation.2 | async-start | bytes 2228224 | tf_op jit(solution)/shard_map/all_to_all | solution.py:450

commit v6 on v5

--- a/solution.py
+++ b/solution.py
@@ -187,8 +187,7 @@
     arrival.wait()
 
     def some(chunk, carry):
-        for kind in range(2):
-            copy(kind, chunk).wait()
+        copy(0, chunk).wait()
         scores, placed, mixed, total = [], [], [], []
         for near in range(group):
             slot = chunk * group + near
@@ -200,6 +199,7 @@
             scores.append(raw + jnp.where(position < length, 0.0, NEG_BIG))
             placed.append((home, first))
         tops = [jnp.max(old, axis=1, keepdims=True) for old in scores]
+        copy(1, chunk).wait()
         for near in range(group):
             terms = jnp.exp2((scores[near] - tops[near]) * (factor * LOG2E))
             total.append(jnp.sum(terms, axis=1, keepdims=True))

time: 109 us -> 109 us (level)
  no operation moved by 1% of the time
where the time goes in v6:
time: 109 us; the launch traced here: 108 us
  waiting for transfers between devices  49.2 us (45%)
  starting transfers between devices  23.8 us (22%)
  Pallas kernels  14.6 us (13%)
  blocking collectives  13.2 us (12%)
  other arithmetic  3.91 us (4%)
  local copies, waits for them, and re-layouts  3.55 us (3%)
    all_to_all x1, waiting for transfers between devices, shards(): back = lax.all_to_all(back, 'lend', split_axis=0, concat_axis=0, tiled=True)  25.3 us
    all_to_all x1, waiting for transfers between devices, shards(): lax.all_to_all(asked, 'lend', split_axis=0, concat_axis=0, tiled=True)  19 us
    all_to_all x1, blocking collectives, shards(): lax.all_to_all(attended, 'tp', split_axis=0, concat_axis=0, tiled=True)  13.2 us
    all_to_all x1, starting transfers between devices, shards(): lax.all_to_all(asked, 'lend', split_axis=0, concat_axis=0, tiled=True)  10.6 us
    pallas_call x1, Pallas kernels, shards(): pl.pallas_call(lambda *refs: lent_kernel(*refs, rows=rows), out_shape=jax...  6.78 us
    all_to_all x1, starting transfers between devices, shards(): lax.all_to_all(packed, 'tp', split_axis=0, concat_axis=0, tiled=True)  6.71 us
    all_to_all x1, starting transfers between devices, shards(): back = lax.all_to_all(back, 'lend', split_axis=0, concat_axis=0, tiled=True)  6.52 us
    all_to_all x1, waiting for transfers between devices, shards(): lax.all_to_all(packed, 'tp', split_axis=0, concat_axis=0, tiled=True)  4.83 us
  transfers between devices with their start and end apart: 3, of which 3 were waited for; matrix products, arithmetic and copies ran while one was open for 4% of the time, Pallas kernels for 3%

profile of v6, /device:TPU:1, one launch (start us, length us, event | category | flops | bytes accessed | tf_op | source)
XLA Modules:
  0.0 108.4 jit_solution(782307127759562966)
XLA Ops:
  0.0 1.7 %pack.1 = bf16[8,144,128]{2,1,0:T(8,128)(2,1)} custom-call(bf16[2,8,64,128]{3,2,1,0:T(8,128)(2,1)} %queries.1, bf16[64,128]{1,0:T(8,128)(2,1)} %bitcast.20, bf16[64,128]{1,0:T(8,128)(2,1)} %bitcast.21), custom_call_target="tpu_custom_call" | custom-call | tf_op jit(solution)/shard_map/pack/pallas_call | solution.py:338
  1.7 0.0 copy-start.5
  1.8 0.0 copy-start.4
  1.8 0.0 copy-start
  1.8 6.7 %all-to-all-start = ((bf16[8,144,128]{2,1,0:T(8,128)(2,1)}), bf16[8,144,128]{2,1,0:T(8,128)(2,1)S(1)}, u32[]{:S(2)}, u32[]{:S(2)}) async-start(bf16[8,144,128]{2,1,0:T(8,128)(2,1)} %pack.1), calls=%async_computation | async-start | bytes 589824 | tf_op jit(solution)/shard_map/all_to_all | solution.py:350
  8.5 0.7 broadcast_subtract_fusion
  9.2 0.1 sub.29
  9.3 0.1 fusion.5
  9.4 0.2 fusion.3
  9.6 0.7 fusion.6
  10.3 0.1 copy.16
  10.4 0.1 stack.14
  10.5 4.8 %all-to-all-done.refs_1_ = bf16[8,144,128]{2,1,0:T(8,128)(2,1)S(1)} async-done(((bf16[8,144,128]{2,1,0:T(8,128)(2,1)}), bf16[8,144,128]{2,1,0:T(8,128)(2,1)S(1)}, u32[]{:S(2)}, u32[]{:S(2)}) %all-to-all-start) | async-done | bytes 294944 | tf_op jit(solution)/shard_map/all_to_all | solution.py:350
  15.3 1.6 %pick.1.refs_5_ = bf16[32,128,128]{2,1,0:T(8,128)(2,1)} custom-call(s32[64]{0:T(128)S(1)} %get-tuple-element.11.refs_0_, bf16[1152,128]{1,0:T(8,128)(2,1)S(1)} %bitcast.14), custom_call_target="tpu_custom_call" | custom-call | tf_op jit(solution)/shard_map/pick/pallas_call | solution.py:389
  16.9 10.6 %all-to-all-start.1 = ((bf16[32,128,128]{2,1,0:T(8,128)(2,1)}), bf16[32,128,128]{2,1,0:T(8,128)(2,1)}, u32[]{:S(2)}, u32[]{:S(2)}) async-start(bf16[32,128,128]{2,1,0:T(8,128)(2,1)} %pick.1.refs_5_), calls=%async_computation.1 | async-start | bytes 2097152 | tf_op jit(solution)/shard_map/all_to_all | solution.py:401
  27.5 0.1 copy.17
  27.6 0.1 broadcast_in_dim.74
  27.7 0.1 reshape.88.refs_4_.refs_1_
  27.8 0.0 copy-done.5
  27.8 0.1 dynamic_slice.7.refs_0_
  27.8 0.0 copy-done.4
  27.8 0.1 fusion.11
  27.9 0.2 convert_reduce_fusion.2
  28.1 0.2 select_reduce_fusion
  28.3 0.2 convert_reduce_fusion
  28.5 0.6 pad_add_fusion.2.refs_0_
  29.1 0.0 copy-done
  29.1 0.0 copy-start.1
  29.1 1.6 %copy-done.1 = bf16[16,512,1,128]{3,1,2,0:T(8,128)(2,1)S(1)} copy-done((bf16[16,512,1,128]{3,1,2,0:T(8,128)(2,1)S(1)}, bf16[16,512,1,128]{3,1,2,0:T(8,128)(2,1)}, u32[]{:S(2)}) %copy-start.1) | copy-done | bytes 2097176
  30.7 2.9 %home.1 = (f32[16,64,128]{2,1,0:T(8,128)S(1)}, f32[16,128]{1,0:T(8,128)S(1)}) custom-call(s32[16]{0:T(128)S(1)} %dynamic_slice.7.refs_0_, bf16[8,144,128]{2,1,0:T(8,128)(2,1)S(1)} %all-to-all-done.refs_1_, bf16[16,512,128]{2,1,0:T(8,128)(2,1)S(1)} %bitcast.15, bf16[16,512,128]{2,1,0:T(8,128)(2,1)S(1)} %bitcast.16, s32[32,128]{1,0:T(8,128)S(1)} %reshape.88.refs_4_.refs_1_, ...), custom_call_target="tpu_custom_call" | custom-call | flops 268435456 | bytes 6291456 | tf_op jit(solution)/shard_map/home/pallas_call | solution.py:403
  33.6 0.0 copy-start.2
  33.6 0.6 copy-done.2
  34.2 19.0 %all-to-all-done.1.refs_1_ = bf16[32,128,128]{2,1,0:T(8,128)(2,1)} async-done(((bf16[32,128,128]{2,1,0:T(8,128)(2,1)}), bf16[32,128,128]{2,1,0:T(8,128)(2,1)}, u32[]{:S(2)}, u32[]{:S(2)}) %all-to-all-start.1) | async-done | bytes 1048608 | tf_op jit(solution)/shard_map/all_to_all | solution.py:401
  53.3 6.8 %lent.1 = bf16[32,136,128]{2,1,0:T(8,128)(2,1)} custom-call(s32[64]{0:T(128)} %pad_add_fusion.2.refs_0_, bf16[32,128,128]{2,1,0:T(8,128)(2,1)} %all-to-all-done.1.refs_1_, bf16[32,512,128]{2,1,0:T(8,128)(2,1)} %bitcast.17, bf16[32,512,128]{2,1,0:T(8,128)(2,1)} %bitcast.18, f32[16,128]{1,0:T(8,128)} %copy-done.2), custom_call_target="tpu_custom_call" | custom-call | tf_op jit(solution)/shard_map/lent/pallas_call | solution.py:429
  60.1 0.0 copy-start.3
  60.1 6.5 %all-to-all-start.2 = ((bf16[32,136,128]{2,1,0:T(8,128)(2,1)}), bf16[32,136,128]{2,1,0:T(8,128)(2,1)S(1)}, u32[]{:S(2)}, u32[]{:S(2)}) async-start(bf16[32,136,128]{2,1,0:T(8,128)(2,1)} %lent.1), calls=%async_computation.2 | async-start | bytes 2228224 | tf_op jit(solution)/shard_map/all_to_all | solution.py:450
  66.6 0.1 convert_reduce_fusion.1
  66.7 0.1 select_reduce_fusion.2
  66.8 0.7 pad_add_fusion.1
  67.5 25.3 %all-to-all-done.2.refs_2_ = bf16[32,136,128]{2,1,0:T(8,128)(2,1)S(1)} async-done(((bf16[32,136,128]{2,1,0:T(8,128)(2,1)}), bf16[32,136,128]{2,1,0:T(8,128)(2,1)S(1)}, u32[]{:S(2)}, u32[]{:S(2)}) %all-to-all-start.2) | async-done | bytes 1114144 | tf_op jit(solution)/shard_map/all_to_all | solution.py:450
  92.9 0.0 copy-done.3
  92.9 1.6 %combine.1 = bf16[8,128,128]{2,1,0:T(8,128)(2,1)S(1)} custom-call(s32[256]{0:T(256)S(1)} %pad.4.refs_0_, s32[32,128]{1,0:T(8,128)S(1)} %reshape.88.refs_4_.refs_1_, bf16[32,136,128]{2,1,0:T(8,128)(2,1)S(1)} %all-to-all-done.2.refs_2_, f32[16,64,128]{2,1,0:T(8,128)S(1)} %get-tuple-element.8.refs_3_, f32[16,128]{1,0:T(8,128)S(1)} %copy-done.3), custom_call_target="tpu_custom_call" | custom-call | tf_op jit(solution)/shard_map/combine/pallas_call | solution.py:452
  94.5 13.2 %all_to_all.20 = bf16[8,128,128]{2,1,0:T(8,128)(2,1)S(1)} all-to-all(bf16[8,128,128]{2,1,0:T(8,128)(2,1)S(1)} %combine.1), channel_id=1, replica_groups=mesh['lend'=32,'tp'=8] {'tp'}, dimensions={0} | all-to-all | bytes 524288 | tf_op jit(solution)/shard_map/all_to_all | solution.py:466
  107.6 0.7 copy.20
  (5 shorter events, 0.0 us)
Async XLA Ops:
  1.7 26.0 %copy-start.5 = (s32[512]{0:T(512)S(1)}, s32[512]{0:T(512)}, u32[]{:S(2)}) copy-start(s32[512]{0:T(512)} %param.16) | copy-start | bytes 6148
  1.8 26.1 %copy-start.4 = (s32[1024]{0:T(1024)S(1)}, s32[1024]{0:T(1024)}, u32[]{:S(2)}) copy-start(s32[1024]{0:T(1024)} %param.17) | copy-start | bytes 12292
  1.8 27.3 %copy-start = (bf16[16,512,1,128]{3,1,2,0:T(8,128)(2,1)S(1)}, bf16[16,512,1,128]{3,1,2,0:T(8,128)(2,1)}, u32[]{:S(2)}) copy-start(bf16[16,512,1,128]{3,1,2,0:T(8,128)(2,1)} %param.12) | copy-start | bytes 6291460
  1.8 13.5 %all-to-all-start = ((bf16[8,144,128]{2,1,0:T(8,128)(2,1)}), bf16[8,144,128]{2,1,0:T(8,128)(2,1)S(1)}, u32[]{:S(2)}, u32[]{:S(2)}) async-start(bf16[8,144,128]{2,1,0:T(8,128)(2,1)} %pack.1), calls=%async_computation | async-start | bytes 589824 | tf_op jit(solution)/shard_map/all_to_all | solution.py:350
  16.9 36.3 %all-to-all-start.1 = ((bf16[32,128,128]{2,1,0:T(8,128)(2,1)}), bf16[32,128,128]{2,1,0:T(8,128)(2,1)}, u32[]{:S(2)}, u32[]{:S(2)}) async-start(bf16[32,128,128]{2,1,0:T(8,128)(2,1)} %pick.1.refs_5_), calls=%async_computation.1 | async-start | bytes 2097152 | tf_op jit(solution)/shard_map/all_to_all | solution.py:401
  29.1 1.6 %copy-start.1 = (bf16[16,512,1,128]{3,1,2,0:T(8,128)(2,1)S(1)}, bf16[16,512,1,128]{3,1,2,0:T(8,128)(2,1)}, u32[]{:S(2)}) copy-start(bf16[16,512,1,128]{3,1,2,0:T(8,128)(2,1)} %param.13) | copy-start | bytes 6291460
  33.6 0.6 copy-start.2
  60.1 32.8 %copy-start.3 = (f32[16,128]{1,0:T(8,128)S(1)}, f32[16,128]{1,0:T(8,128)}, u32[]{:S(2)}) copy-start(f32[16,128]{1,0:T(8,128)} %copy-done.2) | copy-start | bytes 24580
  60.1 32.8 %all-to-all-start.2 = ((bf16[32,136,128]{2,1,0:T(8,128)(2,1)}), bf16[32,136,128]{2,1,0:T(8,128)(2,1)S(1)}, u32[]{:S(2)}, u32[]{:S(2)}) async-start(bf16[32,136,128]{2,1,0:T(8,128)(2,1)} %lent.1), calls=%async_computation.2 | async-start | bytes 2228224 | tf_op jit(solution)/shard_map/all_to_all | solution.py:450

commit v7 on v6

--- a/solution.py
+++ b/solution.py
@@ -15,7 +15,7 @@
 LANES = 128
 LENT_GROUP = 16
 HOME_GROUP = 2
-MERGE_GROUP = 4
+MERGE_GROUP = 8
 LENT_MIB = 58
 
 NEG_BIG = -1e30

time: 109 us -> 109 us (level)
  no operation moved by 1% of the time
where the time goes in v7:
time: 109 us; the launch traced here: 108 us
  waiting for transfers between devices  49.2 us (45%)
  starting transfers between devices  23.8 us (22%)
  Pallas kernels  14.6 us (13%)
  blocking collectives  13.2 us (12%)
  other arithmetic  3.91 us (4%)
  local copies, waits for them, and re-layouts  3.55 us (3%)
    all_to_all x1, waiting for transfers between devices, shards(): back = lax.all_to_all(back, 'lend', split_axis=0, concat_axis=0, tiled=True)  25.3 us
    all_to_all x1, waiting for transfers between devices, shards(): lax.all_to_all(asked, 'lend', split_axis=0, concat_axis=0, tiled=True)  19 us
    all_to_all x1, blocking collectives, shards(): lax.all_to_all(attended, 'tp', split_axis=0, concat_axis=0, tiled=True)  13.2 us
    all_to_all x1, starting transfers between devices, shards(): lax.all_to_all(asked, 'lend', split_axis=0, concat_axis=0, tiled=True)  10.6 us
    pallas_call x1, Pallas kernels, shards(): pl.pallas_call(lambda *refs: lent_kernel(*refs, rows=rows), out_shape=jax...  6.78 us
    all_to_all x1, starting transfers between devices, shards(): lax.all_to_all(packed, 'tp', split_axis=0, concat_axis=0, tiled=True)  6.71 us
    all_to_all x1, starting transfers between devices, shards(): back = lax.all_to_all(back, 'lend', split_axis=0, concat_axis=0, tiled=True)  6.52 us
    all_to_all x1, waiting for transfers between devices, shards(): lax.all_to_all(packed, 'tp', split_axis=0, concat_axis=0, tiled=True)  4.83 us
  transfers between devices with their start and end apart: 3, of which 3 were waited for; matrix products, arithmetic and copies ran while one was open for 4% of the time, Pallas kernels for 3%

profile of v7, /device:TPU:1, one launch (start us, length us, event | category | flops | bytes accessed | tf_op | source)
XLA Modules:
  0.0 108.3 jit_solution(9689111846371751702)
XLA Ops:
  0.0 1.7 %pack.1 = bf16[8,144,128]{2,1,0:T(8,128)(2,1)} custom-call(bf16[2,8,64,128]{3,2,1,0:T(8,128)(2,1)} %queries.1, bf16[64,128]{1,0:T(8,128)(2,1)} %bitcast.20, bf16[64,128]{1,0:T(8,128)(2,1)} %bitcast.21), custom_call_target="tpu_custom_call" | custom-call | tf_op jit(solution)/shard_map/pack/pallas_call | solution.py:338
  1.7 0.0 copy-start.5
  1.8 0.0 copy-start.4
  1.8 0.0 copy-start
  1.8 6.7 %all-to-all-start = ((bf16[8,144,128]{2,1,0:T(8,128)(2,1)}), bf16[8,144,128]{2,1,0:T(8,128)(2,1)S(1)}, u32[]{:S(2)}, u32[]{:S(2)}) async-start(bf16[8,144,128]{2,1,0:T(8,128)(2,1)} %pack.1), calls=%async_computation | async-start | bytes 589824 | tf_op jit(solution)/shard_map/all_to_all | solution.py:350
  8.5 0.7 broadcast_subtract_fusion
  9.2 0.1 sub.29
  9.3 0.1 fusion.5
  9.4 0.2 fusion.3
  9.6 0.7 fusion.6
  10.3 0.1 copy.16
  10.4 0.1 stack.14
  10.5 4.8 %all-to-all-done.refs_1_ = bf16[8,144,128]{2,1,0:T(8,128)(2,1)S(1)} async-done(((bf16[8,144,128]{2,1,0:T(8,128)(2,1)}), bf16[8,144,128]{2,1,0:T(8,128)(2,1)S(1)}, u32[]{:S(2)}, u32[]{:S(2)}) %all-to-all-start) | async-done | bytes 294944 | tf_op jit(solution)/shard_map/all_to_all | solution.py:350
  15.3 1.6 %pick.1.refs_5_ = bf16[32,128,128]{2,1,0:T(8,128)(2,1)} custom-call(s32[64]{0:T(128)S(1)} %get-tuple-element.11.refs_0_, bf16[1152,128]{1,0:T(8,128)(2,1)S(1)} %bitcast.14), custom_call_target="tpu_custom_call" | custom-call | tf_op jit(solution)/shard_map/pick/pallas_call | solution.py:389
  16.9 10.6 %all-to-all-start.1 = ((bf16[32,128,128]{2,1,0:T(8,128)(2,1)}), bf16[32,128,128]{2,1,0:T(8,128)(2,1)}, u32[]{:S(2)}, u32[]{:S(2)}) async-start(bf16[32,128,128]{2,1,0:T(8,128)(2,1)} %pick.1.refs_5_), calls=%async_computation.1 | async-start | bytes 2097152 | tf_op jit(solution)/shard_map/all_to_all | solution.py:401
  27.5 0.1 copy.17
  27.6 0.1 broadcast_in_dim.74
  27.7 0.1 reshape.88.refs_4_.refs_1_
  27.8 0.0 copy-done.5
  27.8 0.1 dynamic_slice.7.refs_0_
  27.8 0.0 copy-done.4
  27.8 0.1 fusion.11
  27.9 0.2 convert_reduce_fusion.2
  28.1 0.2 select_reduce_fusion
  28.3 0.2 convert_reduce_fusion
  28.5 0.6 pad_add_fusion.2.refs_0_
  29.1 0.0 copy-done
  29.1 0.0 copy-start.1
  29.1 1.6 %copy-done.1 = bf16[16,512,1,128]{3,1,2,0:T(8,128)(2,1)S(1)} copy-done((bf16[16,512,1,128]{3,1,2,0:T(8,128)(2,1)S(1)}, bf16[16,512,1,128]{3,1,2,0:T(8,128)(2,1)}, u32[]{:S(2)}) %copy-start.1) | copy-done | bytes 2097176
  30.7 2.9 %home.1 = (f32[16,64,128]{2,1,0:T(8,128)S(1)}, f32[16,128]{1,0:T(8,128)S(1)}) custom-call(s32[16]{0:T(128)S(1)} %dynamic_slice.7.refs_0_, bf16[8,144,128]{2,1,0:T(8,128)(2,1)S(1)} %all-to-all-done.refs_1_, bf16[16,512,128]{2,1,0:T(8,128)(2,1)S(1)} %bitcast.15, bf16[16,512,128]{2,1,0:T(8,128)(2,1)S(1)} %bitcast.16, s32[32,128]{1,0:T(8,128)S(1)} %reshape.88.refs_4_.refs_1_, ...), custom_call_target="tpu_custom_call" | custom-call | flops 268435456 | bytes 6291456 | tf_op jit(solution)/shard_map/home/pallas_call | solution.py:403
  33.6 0.0 copy-start.2
  33.6 0.6 copy-done.2
  34.2 19.0 %all-to-all-done.1.refs_1_ = bf16[32,128,128]{2,1,0:T(8,128)(2,1)} async-done(((bf16[32,128,128]{2,1,0:T(8,128)(2,1)}), bf16[32,128,128]{2,1,0:T(8,128)(2,1)}, u32[]{:S(2)}, u32[]{:S(2)}) %all-to-all-start.1) | async-done | bytes 1048608 | tf_op jit(solution)/shard_map/all_to_all | solution.py:401
  53.3 6.8 %lent.1 = bf16[32,136,128]{2,1,0:T(8,128)(2,1)} custom-call(s32[64]{0:T(128)} %pad_add_fusion.2.refs_0_, bf16[32,128,128]{2,1,0:T(8,128)(2,1)} %all-to-all-done.1.refs_1_, bf16[32,512,128]{2,1,0:T(8,128)(2,1)} %bitcast.17, bf16[32,512,128]{2,1,0:T(8,128)(2,1)} %bitcast.18, f32[16,128]{1,0:T(8,128)} %copy-done.2), custom_call_target="tpu_custom_call" | custom-call | tf_op jit(solution)/shard_map/lent/pallas_call | solution.py:429
  60.1 0.0 copy-start.3
  60.1 6.5 %all-to-all-start.2 = ((bf16[32,136,128]{2,1,0:T(8,128)(2,1)}), bf16[32,136,128]{2,1,0:T(8,128)(2,1)S(1)}, u32[]{:S(2)}, u32[]{:S(2)}) async-start(bf16[32,136,128]{2,1,0:T(8,128)(2,1)} %lent.1), calls=%async_computation.2 | async-start | bytes 2228224 | tf_op jit(solution)/shard_map/all_to_all | solution.py:450
  66.6 0.1 convert_reduce_fusion.1
  66.7 0.1 select_reduce_fusion.2
  66.8 0.7 pad_add_fusion.1
  67.5 25.3 %all-to-all-done.2.refs_2_ = bf16[32,136,128]{2,1,0:T(8,128)(2,1)S(1)} async-done(((bf16[32,136,128]{2,1,0:T(8,128)(2,1)}), bf16[32,136,128]{2,1,0:T(8,128)(2,1)S(1)}, u32[]{:S(2)}, u32[]{:S(2)}) %all-to-all-start.2) | async-done | bytes 1114144 | tf_op jit(solution)/shard_map/all_to_all | solution.py:450
  92.9 0.0 copy-done.3
  92.9 1.5 %combine.1 = bf16[8,128,128]{2,1,0:T(8,128)(2,1)S(1)} custom-call(s32[256]{0:T(256)S(1)} %pad.4.refs_0_, s32[32,128]{1,0:T(8,128)S(1)} %reshape.88.refs_4_.refs_1_, bf16[32,136,128]{2,1,0:T(8,128)(2,1)S(1)} %all-to-all-done.2.refs_2_, f32[16,64,128]{2,1,0:T(8,128)S(1)} %get-tuple-element.8.refs_3_, f32[16,128]{1,0:T(8,128)S(1)} %copy-done.3), custom_call_target="tpu_custom_call" | custom-call | tf_op jit(solution)/shard_map/combine/pallas_call | solution.py:452
  94.4 13.2 %all_to_all.20 = bf16[8,128,128]{2,1,0:T(8,128)(2,1)S(1)} all-to-all(bf16[8,128,128]{2,1,0:T(8,128)(2,1)S(1)} %combine.1), channel_id=1, replica_groups=mesh['lend'=32,'tp'=8] {'tp'}, dimensions={0} | all-to-all | bytes 524288 | tf_op jit(solution)/shard_map/all_to_all | solution.py:466
  107.6 0.7 copy.20
  (5 shorter events, 0.0 us)
Async XLA Ops:
  1.7 26.0 %copy-start.5 = (s32[512]{0:T(512)S(1)}, s32[512]{0:T(512)}, u32[]{:S(2)}) copy-start(s32[512]{0:T(512)} %param.16) | copy-start | bytes 6148
  1.8 26.1 %copy-start.4 = (s32[1024]{0:T(1024)S(1)}, s32[1024]{0:T(1024)}, u32[]{:S(2)}) copy-start(s32[1024]{0:T(1024)} %param.17) | copy-start | bytes 12292
  1.8 27.3 %copy-start = (bf16[16,512,1,128]{3,1,2,0:T(8,128)(2,1)S(1)}, bf16[16,512,1,128]{3,1,2,0:T(8,128)(2,1)}, u32[]{:S(2)}) copy-start(bf16[16,512,1,128]{3,1,2,0:T(8,128)(2,1)} %param.12) | copy-start | bytes 6291460
  1.8 13.5 %all-to-all-start = ((bf16[8,144,128]{2,1,0:T(8,128)(2,1)}), bf16[8,144,128]{2,1,0:T(8,128)(2,1)S(1)}, u32[]{:S(2)}, u32[]{:S(2)}) async-start(bf16[8,144,128]{2,1,0:T(8,128)(2,1)} %pack.1), calls=%async_computation | async-start | bytes 589824 | tf_op jit(solution)/shard_map/all_to_all | solution.py:350
  16.9 36.3 %all-to-all-start.1 = ((bf16[32,128,128]{2,1,0:T(8,128)(2,1)}), bf16[32,128,128]{2,1,0:T(8,128)(2,1)}, u32[]{:S(2)}, u32[]{:S(2)}) async-start(bf16[32,128,128]{2,1,0:T(8,128)(2,1)} %pick.1.refs_5_), calls=%async_computation.1 | async-start | bytes 2097152 | tf_op jit(solution)/shard_map/all_to_all | solution.py:401
  29.1 1.6 %copy-start.1 = (bf16[16,512,1,128]{3,1,2,0:T(8,128)(2,1)S(1)}, bf16[16,512,1,128]{3,1,2,0:T(8,128)(2,1)}, u32[]{:S(2)}) copy-start(bf16[16,512,1,128]{3,1,2,0:T(8,128)(2,1)} %param.13) | copy-start | bytes 6291460
  33.6 0.6 copy-start.2
  60.1 32.8 %copy-start.3 = (f32[16,128]{1,0:T(8,128)S(1)}, f32[16,128]{1,0:T(8,128)}, u32[]{:S(2)}) copy-start(f32[16,128]{1,0:T(8,128)} %copy-done.2) | copy-start | bytes 24580
  60.1 32.8 %all-to-all-start.2 = ((bf16[32,136,128]{2,1,0:T(8,128)(2,1)}), bf16[32,136,128]{2,1,0:T(8,128)(2,1)S(1)}, u32[]{:S(2)}, u32[]{:S(2)}) async-start(bf16[32,136,128]{2,1,0:T(8,128)(2,1)} %lent.1), calls=%async_computation.2 | async-start | bytes 2228224 | tf_op jit(solution)/shard_map/all_to_all | solution.py:450
